TPU v7x, 512 devices: a whole 4x4x16 slice. The times are simulated.
512 devices in a mesh: dp: 64 (over z_lo, y, x), mp: 8 (over z_hi, core).
Axes of the slice: x: 4, y: 4, z: 16 (z_hi: 4, z_lo: 4; z = z_hi * 4 + z_lo), core: 2. Of those that a mesh axis runs over, the one named last changes fastest.
Arguments:
- inputs: bfloat16 [8192, 5120], P('dp', 'mp'), may hold values from -6 to 6
- upstream: bfloat16 [8192, 5120], P('dp', 'mp'), may hold values from -0.796875 to 0.796875
- master: float32 [3, 512, 5120], P(None, 'mp', 'dp'), may hold values from -0.078125 to 0.078125
- moment_one: float32 [3, 512, 5120], P(None, 'mp', 'dp'), may hold values from -6 to 6
- moment_two: float32 [3, 512, 5120], P(None, 'mp', 'dp'), may hold values from 1 to 100
Outputs:
- master_new: float32 [3, 512, 5120], P(None, 'mp', 'dp')
- moment_one_new: float32 [3, 512, 5120], P(None, 'mp', 'dp')
- moment_two_new: float32 [3, 512, 5120], P(None, 'mp', 'dp')
- weights_new: bfloat16 [3, 512, 5120], P(None, 'mp')
All inputs are finite; a program needn't handle non-finite values.
Results may differ from a plain program's by a relative error of at most 0.001.
Values may be sent and summed in bfloat16 or wider, within the bound.
A program may use at most 64 MiB of HBM per device.

v0:
```python
import jax
import jax.numpy as jnp
from jax import lax
from jax.sharding import PartitionSpec as P

beta_one = 0.9
beta_two = 0.95
learn_rate = 0.0003
decay_rate = 0.1
eps_small = 1e-08
corr_one = 1.0 - 0.9**40
corr_two = 1.0 - 0.95**40


def contract_tokens(left, right):
    return lax.dot_general(
        left, right, (((0,), (0,)), ((), ())), preferred_element_type=jnp.float32
    )


def contract_width(left, right):
    return lax.dot_general(
        left, right, (((1,), (1,)), ((), ())), preferred_element_type=jnp.float32
    )


def local(inputs, upstream, master, moment_one, moment_two):
    acts_full, cotan_full = (
        lax.all_gather(inputs, "mp", axis=1, tiled=True),
        lax.all_gather(upstream, "mp", axis=1, tiled=True),
    )
    piece = lax.all_gather(master.astype(jnp.bfloat16), "dp", axis=2, tiled=True)
    gate = contract_width(acts_full, piece[0])
    upval = contract_width(acts_full, piece[1])
    dhidden = contract_width(cotan_full, piece[2])
    sigma = jax.nn.sigmoid(gate)
    hidden = (gate * sigma * upval).astype(jnp.bfloat16)
    dgate = (dhidden * upval * sigma * (1.0 + gate * (1.0 - sigma))).astype(jnp.bfloat16)
    dup = (dhidden * gate * sigma).astype(jnp.bfloat16)
    grads_all = jnp.stack(
        [
            contract_tokens(dgate, acts_full),
            contract_tokens(dup, acts_full),
            contract_tokens(hidden, cotan_full),
        ]
    )
    grads = lax.psum_scatter(grads_all, "dp", scatter_dimension=2, tiled=True)
    first = beta_one * moment_one + (1.0 - beta_one) * grads
    second = beta_two * moment_two + (1.0 - beta_two) * grads * grads
    update = first / corr_one / (jnp.sqrt(second / corr_two) + eps_small)
    master_new = master - learn_rate * (update + decay_rate * master)
    gathered = lax.all_gather(master_new.astype(jnp.bfloat16), "dp", axis=2, tiled=True)
    return (master_new, first, second, gathered)


def solution(mesh):
    placed = (
        P("dp", "mp"),
        P("dp", "mp"),
        P(None, "mp", "dp"),
        P(None, "mp", "dp"),
        P(None, "mp", "dp"),
    )
    return jax.shard_map(
        local,
        mesh=mesh,
        in_specs=placed,
        out_specs=(
            P(None, "mp", "dp"),
            P(None, "mp", "dp"),
            P(None, "mp", "dp"),
            P(None, "mp", None),
        ),
        check_vma=False,
    )
```

profile of v0, /device:TPU:4, one launch (start us, length us, event | category | flops | bytes accessed | tf_op | source)
XLA Modules:
  0.0 1256.2 jit_solution(13988608642837961222)
XLA Ops:
  7.2 0.0 all-gather.7.cloned.1.call-start
  7.2 0.9 convert_element_type.15
  8.1 0.7 copy.18
  8.9 0.0 all-gather.7.cloned.1.call-update
  8.9 0.0 all-gather.9.cloned.1.call-start
  8.9 0.7 all-gather.9.cloned.1.call-update
  9.6 0.0 all-gather.5.cloned.1.call-start
  9.7 0.7 all-gather.5.cloned.1.call-update
  10.4 0.0 reduce-scatter.4.cloned.1.call-start
  10.4 364.5 %all-gather.7.cloned.1.call-done = bf16[3,64,5120]{1,0,2:T(4,128)(2,1)} async-done(((bf16[3,64,80]{1,0,2:T(4,128)(2,1)}), bf16[3,64,5120]{1,0,2:T(4,128)(2,1)}) %all-gather.7.cloned.1.call-update) | async-done | bytes 1966096 | tf_op jit(solution)/shard_map/all_gather | solution.py:32
  374.9 13.3 %fusion.15 = (bf16[1,64,5120]{1,0,2:T(2,128)(2,1)S(1)}, bf16[1,64,5120]{1,0,2:T(2,128)(2,1)}, bf16[1,64,5120]{1,0,2:T(2,128)(2,1)}) fusion(bf16[3,64,5120]{1,0,2:T(4,128)(2,1)} %all-gather.7.cloned.1.call-done), kind=kLoop, calls=%fused_computation.25 | loop fusion | bytes 3932160 | tf_op jit(solution)/shard_map/slice | solution.py:35
  388.2 5.9 copy.28
  394.1 5.9 copy.27
  400.0 1.5 copy.26
  401.5 0.0 copy-start.2
  401.5 26.6 %all-gather.9.cloned.1.call-done = bf16[128,5120]{1,0:T(8,128)(2,1)} async-done(((bf16[128,640]{1,0:T(8,128)(2,1)}), bf16[128,5120]{1,0:T(8,128)(2,1)}) %all-gather.9.cloned.1.call-update) | async-done | bytes 1310736 | tf_op jit(solution)/shard_map/all_gather | solution.py:29
  428.1 0.0 copy-start
  428.1 2.2 fusion
  430.2 0.0 copy-done.2
  430.2 0.0 copy-done
  430.3 0.6 fusion.2
  430.8 45.9 %all-gather.5.cloned.1.call-done = bf16[128,5120]{1,0:T(8,128)(2,1)} async-done(((bf16[128,640]{1,0:T(8,128)(2,1)}), bf16[128,5120]{1,0:T(8,128)(2,1)}) %all-gather.5.cloned.1.call-update) | async-done | bytes 1310736 | tf_op jit(solution)/shard_map/all_gather | solution.py:30
  476.7 1.9 fusion.4
  478.6 0.3 convolution_bitcast_fusion.1
  478.9 0.0 copy-start.1
  478.9 0.3 convolution_bitcast_fusion.2
  479.3 1.0 copy-done.1
  480.3 0.3 convolution_bitcast_fusion
  480.6 2.4 pad_maximum_fusion
  483.0 9.0 copy.24
  491.9 12.5 reshape.8
  504.4 0.0 copy-start.3
  504.4 0.0 copy-start.4
  504.4 0.0 copy-start.5
  504.4 0.0 reduce-scatter.4.cloned.1.call-update
  504.4 0.0 all-gather.11.cloned.1.call-start
  504.5 374.6 %reduce-scatter.4.cloned.1.call-done = f32[80,192]{1,0:T(8,128)} async-done(((f32[5120,192]{1,0:T(8,128)}), f32[80,192]{1,0:T(8,128)}) %reduce-scatter.4.cloned.1.call-update) | async-done | bytes 61456
  879.1 1.0 reshape.9
  880.1 0.1 copy.25
  880.2 0.0 copy-done.3
  880.2 0.0 copy-done.4
  880.2 0.0 copy-done.5
  880.2 0.8 fusion.13
  881.0 0.7 copy.22
  881.7 0.0 all-gather.11.cloned.1.call-update
  881.7 360.8 %all-gather.11.cloned.1.call-done = bf16[3,64,5120]{1,0,2:T(4,128)(2,1)} async-done(((bf16[3,64,80]{1,0,2:T(4,128)(2,1)}), bf16[3,64,5120]{1,0,2:T(4,128)(2,1)}) %all-gather.11.cloned.1.call-update) | async-done | bytes 1966096 | tf_op jit(solution)/shard_map/all_gather | solution.py:52
  1242.5 7.1 copy.23
Async XLA Ops:
  7.2 367.8 %all-gather.7.cloned.1.call-start = ((), (), s32[]{:S(2)}) async-start(), calls=%async_computation.2 | async-start | bytes 5324800 | tf_op jit(solution)/shard_map/all_gather | solution.py:32
  8.9 419.2 %all-gather.9.cloned.1.call-start = ((), (), s32[]{:S(2)}) async-start(), calls=%async_computation.3 | async-start | bytes 1474560 | tf_op jit(solution)/shard_map/all_gather | solution.py:29
  9.6 467.1 %all-gather.5.cloned.1.call-start = ((), (), s32[]{:S(2)}) async-start(), calls=%async_computation.1 | async-start | bytes 1474560 | tf_op jit(solution)/shard_map/all_gather | solution.py:30
  10.4 868.7 %reduce-scatter.4.cloned.1.call-start = ((), (), s32[]{:S(2)}) async-start(), calls=%async_computation.5 | async-start | bytes 5324800
  401.5 28.7 %copy-start.2 = (bf16[1,64,5120]{2,1,0:T(8,128)(2,1)S(1)}, bf16[1,64,5120]{2,1,0:T(8,128)(2,1)}, u32[]{:S(2)}) copy-start(bf16[1,64,5120]{2,1,0:T(8,128)(2,1)} %copy.27) | copy-start | bytes 1966084
  428.1 2.2 copy-start
  478.9 1.3 copy-start.1
  504.4 375.8 %copy-start.3 = (f32[3,64,80]{2,1,0:T(8,128)S(1)}, f32[3,64,80]{2,1,0:T(8,128)}, u32[]{:S(2)}) copy-start(f32[3,64,80]{2,1,0:T(8,128)} %param.7) | copy-start | bytes 184324
  504.4 375.8 %copy-start.4 = (f32[3,64,80]{2,1,0:T(8,128)S(1)}, f32[3,64,80]{2,1,0:T(8,128)}, u32[]{:S(2)}) copy-start(f32[3,64,80]{2,1,0:T(8,128)} %param.8) | copy-start | bytes 184324
  504.4 375.8 %copy-start.5 = (f32[3,64,80]{2,1,0:T(8,128)S(1)}, f32[3,64,80]{2,1,0:T(8,128)}, u32[]{:S(2)}) copy-start(f32[3,64,80]{2,1,0:T(8,128)} %param.9) | copy-start | bytes 184324
  504.4 738.1 %all-gather.11.cloned.1.call-start = ((), (), s32[]{:S(2)}) async-start(), calls=%async_computation.4 | async-start | bytes 5324800 | tf_op jit(solution)/shard_map/all_gather | solution.py:52
Sparse Core Ops, SparseCore 0:
  10.7 364.2 all-gather.6
  377.1 50.9 all-gather.8
  430.2 46.4 all-gather.4
  504.6 374.4 reduce-scatter.3
  881.9 360.6 all-gather.10
where the time goes:
time: 1260 us
  waiting for transfers between devices  1170 us (93%)
  local copies, waits for them, and re-layouts  58.7 us (5%)
  between operations  13.9 us (1%)
    unnamed x6, waiting for transfers between devices  376 us
    all_gather x1, waiting for transfers between devices, local(): lax.all_gather(master.astype(jnp.bfloat16), 'dp', axis=2, tiled=True)  365 us
    all_gather x1, waiting for transfers between devices, local(): lax.all_gather(master_new.astype(jnp.bfloat16), 'dp', axis=2, tiled=True)  361 us
    all_gather x1, waiting for transfers between devices, local(): lax.all_gather(upstream, 'mp', axis=1, tiled=True)  45.9 us
    unnamed x20, local copies, waits for them, and re-layouts  43.9 us
    all_gather x1, waiting for transfers between devices, local(): lax.all_gather(inputs, 'mp', axis=1, tiled=True)  26.6 us
  transfers between devices with their start and end apart: 5, of which 5 were waited for; matrix products, arithmetic and copies ran while one was open for 2% of the time, Pallas kernels for 0%

commit v1 on v0

v1 whole, which is shorter than its diff:
```python
import functools

import jax
import jax.numpy as jnp
from jax import lax
from jax.experimental import pallas as pl
from jax.experimental.pallas import tpu as pltpu
from jax.sharding import PartitionSpec as P

beta_one = 0.9
beta_two = 0.95
learn_rate = 0.0003
decay_rate = 0.1
eps_small = 1e-08
corr_one = 1.0 - 0.9**40
corr_two = 1.0 - 0.95**40

MESH = pl.DeviceIdType.MESH
f32 = jnp.float32
bf16 = jnp.bfloat16
N_COPIES = 64


def kernel(
    stop,
    inputs, upstream, master, moment_one, moment_two,
    master_new, first_new, second_new, weights_new,
    feats, wown, wbuf, part, core_in, quarter, rs_half, rs_full, dcat,
    featT, gbuf, gy_half, gy_full, gline, gz_in, g01, g2, aline, fin,
    send_sems, recv_sems,
):
    i, j = lax.axis_index("dp"), lax.axis_index("mp")
    z, y, x = i // 16, (i // 4) % 4, i % 4
    zh, core = j // 2, j % 2

    def dev(zh=zh, core=core, z=z, y=y, x=x):
        return (z * 16 + y * 4 + x, zh * 2 + core)

    right, left = dev(x=(x + 1) % 4), dev(x=(x + 3) % 4)
    up, down = dev(y=(y + 1) % 4), dev(y=(y + 3) % 4)
    line = [None] + [dev(z=(z + k) % 4) for k in (1, 2, 3)]
    above, below = dev(zh=(zh + 1) % 4), dev(zh=(zh + 3) % 4)
    mate = dev(core=1 - core)
    holder = dev(zh=z, core=y // 2, z=x, y=2 * core + 1 - y % 2, x=zh)
    holder_b = dev(zh=z, core=y // 2, z=x, y=2 * (1 - core) + 1 - y % 2, x=zh)
    owner = dev(zh=x, core=y // 2, z=zh, y=2 * core + 1 - y % 2, x=z)
    owner_b = dev(zh=x, core=1 - y // 2, z=zh, y=2 * core + 1 - y % 2, x=z)
    slot = lambda v: v + 1 - 2 * (v % 2)
    yu, yd, y2 = (y + 1) % 4, (y + 3) % 4, (y + 2) % 4
    zu, zd, z2 = (zh + 1) % 4, (zh + 3) % 4, (zh + 2) % 4

    started = []

    def put(src, dst, to):
        k = len(started)
        copy = pltpu.make_async_remote_copy(
            src_ref=src, dst_ref=dst, send_sem=send_sems.at[k], recv_sem=recv_sems.at[k],
            device_id=to, device_id_type=MESH,
        )
        copy.start()
        started.append(copy)
        return copy

    def finish():
        for copy in started:
            copy.wait_send()

    barrier = pltpu.get_barrier_semaphore()
    greeted = [right, left, up, down, *line[1:], above, below, mate, holder, holder_b, owner, owner_b]
    for other in greeted:
        pl.semaphore_signal(barrier, inc=1, device_id=other, device_id_type=MESH)

    feats[0, 0] = inputs[...]
    feats[1, 0] = upstream[...]
    low = lax.broadcasted_iota(jnp.int32, (80, 128), 1) < 64
    rows = master[...].reshape(192, 80)
    wown[0:80, :] = rows[0:128].T.astype(bf16)
    down_rows = jnp.concatenate([rows[128:192], rows[128:192]], axis=0).T
    wown[80:160, :] = jnp.where(low == (core == 0), down_rows, 0.0).astype(bf16)

    pl.semaphore_wait(barrier, len(greeted))

    c_w = put(wown, wbuf.at[2 * core + y % 2, x], holder)
    c_r = [put(feats.at[n, 0], feats.at[n, 3], right) for n in (0, 1)]
    c_l = [put(feats.at[n, 0], feats.at[n, 1], left) for n in (1, 0)]

    c_w.wait_recv()
    mine = wbuf.at[slot(y), z]
    c_z = [put(mine, mine, line[k]) for k in (1, 2, 3)]
    for c in c_z:
        c.wait_recv()
    mine = wbuf.at[slot(y)]
    c_u = put(mine, mine, up)
    c_d = put(mine, mine, down)
    c_r[0].wait_recv()
    c_r2 = put(feats.at[0, 3], feats.at[0, 2], right)
    c_l[0].wait_recv()
    c_l2 = put(feats.at[1, 1], feats.at[1, 2], left)
    c_u.wait_recv()
    piece = wbuf.at[slot(yd), pl.ds(0, 2)]
    c_u2 = put(piece, piece, up)
    c_d.wait_recv()
    piece = wbuf.at[slot(yu), pl.ds(2, 2)]
    c_d2 = put(piece, piece, down)
    for c in (c_r[1], c_l[1], c_r2, c_l2, c_u2, c_d2):
        c.wait_recv()
    if stop == 1:
        return finish()

    w01 = [wbuf[2 * b : 2 * b + 2, :, 0:80, :].reshape(640, 128) for b in (0, 1)]
    w01 = jnp.concatenate(w01, axis=1)
    w2 = (wbuf[0:2, :, 80:160, :] + wbuf[2:4, :, 80:160, :]).reshape(640, 128)
    for half in (0, 1):
        a = feats[0, 2 * half : 2 * half + 2].reshape(256, 640)
        u = feats[1, 2 * half : 2 * half + 2].reshape(256, 640)
        part[half, :, 0:256] = jnp.dot(a, w01, preferred_element_type=f32)
        part[half, :, 256:384] = jnp.dot(u, w2, preferred_element_type=f32)

    c_m = put(part.at[1 - core], core_in, mate)
    for n in (0, 1):
        featT[n] = feats[n].reshape(512, 640).T
    c_m.wait_recv()
    quarter[...] = (part[core] + core_in[...]).reshape(4, 64, 384)
    lo, hi = pl.ds(0, 32), pl.ds(32, 32)
    c_a1 = put(quarter.at[z2, lo], rs_half.at[0], above)
    c_b1 = put(quarter.at[z2, hi], rs_half.at[1], below)
    c_a2 = put(quarter.at[zu, hi], rs_full.at[0, hi], above)
    c_b2 = put(quarter.at[zd, lo], rs_full.at[1, lo], below)
    c_a1.wait_recv()
    quarter[zu, 0:32] += rs_half[0]
    c_a3 = put(quarter.at[zu, lo], rs_full.at[0, lo], above)
    c_b1.wait_recv()
    quarter[zd, 32:64] += rs_half[1]
    c_b3 = put(quarter.at[zd, hi], rs_full.at[1, hi], below)
    for c in (c_a2, c_b2, c_a3, c_b3):
        c.wait_recv()
    if stop == 2:
        return finish()

    total = quarter[zh] + rs_full[0] + rs_full[1]
    t0, t1, dhidden = total[:, 0:128], total[:, 128:256], total[:, 256:384]
    low = lax.broadcasted_iota(jnp.int32, (64, 128), 1) < 64
    gate = jnp.where(low, t0, pltpu.roll(t1, 64, 1))
    upval = jnp.where(low, pltpu.roll(t0, 64, 1), t1)
    sigma = jax.nn.sigmoid(gate)
    hidden = gate * sigma * upval
    dgate = dhidden * upval * sigma * (1.0 + gate * (1.0 - sigma))
    dup = dhidden * gate * sigma
    dcat[core, zh, :, 0:128] = jnp.where(low, dgate, pltpu.roll(dup, 64, 1)).astype(bf16)
    dcat[core, zh, :, 128:256] = jnp.where(low, pltpu.roll(dgate, 64, 1), dup).astype(bf16)
    dcat[core, zh, :, 256:384] = hidden.astype(bf16)

    mine = dcat.at[core, zh]
    c_a = put(mine, mine, above)
    c_b = put(mine, mine, below)
    c_m = [put(mine, mine, mate)]
    c_a.wait_recv()
    piece = dcat.at[core, zd, lo]
    c_a2 = put(piece, piece, above)
    c_b.wait_recv()
    piece = dcat.at[core, zu, hi]
    c_b2 = put(piece, piece, below)
    for v in (zd, zu):
        piece = dcat.at[core, v]
        c_m.append(put(piece, piece, mate))
    c_a2.wait_recv()
    c_b2.wait_recv()
    piece = dcat.at[core, z2]
    c_m.append(put(piece, piece, mate))
    for c in c_m:
        c.wait_recv()
    if stop == 3:
        return finish()

    d01 = dcat[:, :, :, 0:256].reshape(512, 256)
    d2 = dcat[:, :, :, 256:384].reshape(512, 128)
    for s in range(8):
        span = slice(80 * s, 80 * s + 80)
        p01 = jnp.dot(featT[0, span, :], d01, preferred_element_type=f32)
        p2 = jnp.dot(featT[1, span, :], d2, preferred_element_type=f32)
        for b in (0, 1):
            gbuf[2 * b + s // 4, s % 4, 0:80, :] = p01[:, 128 * b : 128 * b + 128]
            gbuf[2 * b + s // 4, s % 4, 80:120, :] = p2[40 * b : 40 * b + 40]

    lo, hi = pl.ds(0, 2), pl.ds(2, 2)
    c_a1 = put(gbuf.at[slot(y2), lo], gy_half.at[0], up)
    c_b1 = put(gbuf.at[slot(y2), hi], gy_half.at[1], down)
    c_a2 = put(gbuf.at[slot(yu), hi], gy_full.at[0, hi], up)
    c_b2 = put(gbuf.at[slot(yd), lo], gy_full.at[1, lo], down)
    c_a1.wait_recv()
    gbuf[slot(yu), 0:2] += gy_half[0]
    c_a3 = put(gbuf.at[slot(yu), lo], gy_full.at[0, lo], up)
    c_b1.wait_recv()
    gbuf[slot(yd), 2:4] += gy_half[1]
    c_b3 = put(gbuf.at[slot(yd), hi], gy_full.at[1, hi], down)
    for c in (c_a2, c_b2, c_a3, c_b3):
        c.wait_recv()
    if stop == 4:
        return finish()
    gline[...] = gbuf[slot(y)] + gy_full[0] + gy_full[1]
    c_z = [put(gline.at[(z + k) % 4], gz_in.at[k - 1], line[k]) for k in (1, 2, 3)]
    for c in c_z:
        c.wait_recv()
    gline[z] += gz_in[0] + gz_in[1] + gz_in[2]
    if stop == 5:
        return finish()

    c_1 = put(gline.at[z, pl.ds(0, 80)], g01, owner)
    c_2 = put(gline.at[z, pl.ds(80, 40)], g2.at[y // 2], owner)
    c_3 = put(gline.at[z, pl.ds(80, 40)], g2.at[y // 2], owner_b)
    for c in (c_1, c_2, c_3):
        c.wait_recv()
    if stop == 6:
        return finish()

    down_grads = g2[...].reshape(80, 128).T
    down_grads = jnp.where(core == 0, down_grads[0:64], down_grads[64:128])
    grads = jnp.concatenate([g01[...].T, down_grads], axis=0).reshape(3, 64, 80)
    first = beta_one * moment_one[...] + (1.0 - beta_one) * grads
    second = beta_two * moment_two[...] + (1.0 - beta_two) * grads * grads
    update = first / corr_one / (jnp.sqrt(second / corr_two) + eps_small)
    fresh = master[...] - learn_rate * (update + decay_rate * master[...])
    first_new[...] = first
    second_new[...] = second
    master_new[...] = fresh
    fresh = fresh.reshape(192, 80)
    aline[z, 0:80, :] = fresh[0:128].T.astype(bf16)
    down_rows = jnp.concatenate([fresh[128:192], jnp.zeros((64, 80), f32)], axis=0).T
    aline[z, 80:160, :] = down_rows.astype(bf16)

    mine = aline.at[z]
    c_z = [put(mine, mine, line[k]) for k in (1, 2, 3)]
    for c in c_z:
        c.wait_recv()
    fin[y, x, 0:320, :] = aline[:, 0:80, :].reshape(320, 128)
    tail = aline[:, 80:160, :].astype(f32)
    packed = tail[0:2].reshape(160, 128) + pltpu.roll(tail[2:4].reshape(160, 128), 64, 1)
    fin[y, x, 320:480, :] = packed.astype(bf16)
    if stop == 7:
        return finish()

    xu, xd = (x + 1) % 4, (x + 3) % 4
    a_all, b_all = pl.ds(0, 240), pl.ds(240, 240)
    mine_a, mine_b = fin.at[y, x, a_all], fin.at[y, x, b_all]
    c_ar, c_al = put(mine_a, mine_a, right), put(mine_a, mine_a, left)
    c_bu, c_bd = put(mine_b, mine_b, up), put(mine_b, mine_b, down)
    c_ar.wait_recv()
    piece = fin.at[y, xd, pl.ds(0, 128)]
    c_ar2 = put(piece, piece, right)
    c_al.wait_recv()
    piece = fin.at[y, xu, pl.ds(128, 112)]
    c_al2 = put(piece, piece, left)
    c_bu.wait_recv()
    piece = fin.at[yd, x, pl.ds(240, 128)]
    c_bu2 = put(piece, piece, up)
    c_bd.wait_recv()
    piece = fin.at[yu, x, pl.ds(368, 112)]
    c_bd2 = put(piece, piece, down)
    for c in (c_ar2, c_al2, c_bu2, c_bd2):
        c.wait_recv()
    if stop == 8:
        return finish()
    mine_a, mine_b = fin.at[y, :, a_all], fin.at[:, x, b_all]
    c_au, c_ad = put(mine_a, mine_a, up), put(mine_a, mine_a, down)
    c_br, c_bl = put(mine_b, mine_b, right), put(mine_b, mine_b, left)
    c_au.wait_recv()
    piece = fin.at[yd, pl.ds(0, 2), a_all]
    c_au2 = put(piece, piece, up)
    c_br.wait_recv()
    piece = fin.at[pl.ds(0, 2), xd, b_all]
    c_br2 = put(piece, piece, right)
    c_ad.wait_recv()
    piece = fin.at[yu, pl.ds(2, 2), a_all]
    c_ad2 = put(piece, piece, down)
    c_bl.wait_recv()
    piece = fin.at[pl.ds(2, 2), xu, b_all]
    c_bl2 = put(piece, piece, left)
    for c in (c_au2, c_ad2, c_br2, c_bl2):
        c.wait_recv()
    if stop == 9:
        return finish()

    for n in range(4):
        cols = slice(1280 * n, 1280 * n + 1280)
        block = fin[:, :, 80 * n : 80 * n + 80, :].reshape(1280, 128).T
        weights_new[0, :, cols] = block[0:64]
        weights_new[1, :, cols] = block[64:128]
    for n in range(2):
        block = fin[:, :, 320 + 80 * n : 400 + 80 * n, :].reshape(1280, 128).T
        weights_new[2, :, 1280 * n : 1280 * n + 1280] = block[0:64]
        weights_new[2, :, 1280 * (n + 2) : 1280 * (n + 3)] = block[64:128]
    finish()


def local(stop, inputs, upstream, master, moment_one, moment_two):
    shard = jax.ShapeDtypeStruct((3, 64, 80), f32)
    vmem = pl.BlockSpec(memory_space=pltpu.VMEM)
    return pl.pallas_call(
        functools.partial(kernel, stop),
        out_shape=(shard, shard, shard, jax.ShapeDtypeStruct((3, 64, 5120), bf16)),
        in_specs=[vmem] * 5,
        out_specs=(vmem,) * 4,
        scratch_shapes=[
            pltpu.VMEM((2, 4, 128, 640), bf16),
            pltpu.VMEM((160, 128), bf16),
            pltpu.VMEM((4, 4, 160, 128), bf16),
            pltpu.VMEM((2, 256, 384), f32),
            pltpu.VMEM((256, 384), f32),
            pltpu.VMEM((4, 64, 384), f32),
            pltpu.VMEM((2, 32, 384), f32),
            pltpu.VMEM((2, 64, 384), f32),
            pltpu.VMEM((2, 4, 64, 384), bf16),
            pltpu.VMEM((2, 640, 512), bf16),
            pltpu.VMEM((4, 4, 120, 128), f32),
            pltpu.VMEM((2, 2, 120, 128), f32),
            pltpu.VMEM((2, 4, 120, 128), f32),
            pltpu.VMEM((4, 120, 128), f32),
            pltpu.VMEM((3, 120, 128), f32),
            pltpu.VMEM((80, 128), f32),
            pltpu.VMEM((2, 40, 128), f32),
            pltpu.VMEM((4, 160, 128), bf16),
            pltpu.VMEM((4, 4, 480, 128), bf16),
            pltpu.SemaphoreType.DMA((N_COPIES,)),
            pltpu.SemaphoreType.DMA((N_COPIES,)),
        ],
        compiler_params=pltpu.CompilerParams(
            collective_id=0, has_side_effects=True, vmem_limit_bytes=40 * 2**20
        ),
        cost_estimate=pl.CostEstimate(
            flops=503316480, bytes_accessed=8000000, transcendentals=8192
        ),
        name="fused_step",
    )(inputs, upstream, master, moment_one, moment_two)


def solution(mesh, stop=0):
    owned = P(None, "mp", "dp")
    return jax.shard_map(
        functools.partial(local, stop),
        mesh=mesh,
        in_specs=(P("dp", "mp"), P("dp", "mp"), owned, owned, owned),
        out_specs=(owned, owned, owned, P(None, "mp", None)),
        check_vma=False,
    )
```

time: 1260 us -> 138 us (0.11)
  the two profiles are of different devices: /device:TPU:4 before, /device:TPU:2 now
where the time goes in v1:
time: 138 us
  Pallas kernels  130 us (94%)
  local copies, waits for them, and re-layouts  7.69 us (6%)
    pallas_call x1, Pallas kernels, local(): pl.pallas_call(functools.partial(kernel, stop), out_shape=(shard, shard,...  130 us
    unnamed x14, local copies, waits for them, and re-layouts  7.69 us

profile of v1, /device:TPU:2, one launch (start us, length us, event | category | flops | bytes accessed | tf_op | source)
XLA Modules:
  0.0 138.2 jit_solution(2255774307762132857)
XLA Ops:
  0.6 0.0 copy-start
  0.6 0.9 copy-done
  1.5 0.0 copy-start.1
  1.6 0.9 copy-done.1
  2.5 0.0 copy-start.2
  2.5 0.9 copy-done.2
  3.4 0.0 copy-start.3
  3.4 0.9 copy-done.3
  4.3 0.0 copy-start.4
  4.3 0.9 copy-done.4
  5.1 129.8 %fused_step.1 = (f32[3,64,80]{2,1,0:T(8,128)S(1)}, f32[3,64,80]{2,1,0:T(8,128)S(1)}, f32[3,64,80]{2,1,0:T(8,128)S(1)}, bf16[3,64,5120]{2,1,0:T(8,128)(2,1)S(1)}) custom-call(bf16[128,640]{1,0:T(8,128)(2,1)S(1)} %copy-done, bf16[128,640]{1,0:T(8,128)(2,1)S(1)} %copy-done.1, f32[3,64,80]{2,1,0:T(8,128)S(1)} %copy-done.2, f32[3,64,80]{2,1,0:T(8,128)S(1)} %copy-done.3, ...), custom_call_target="tpu_custom_call" | custom-call | flops 503316480 | bytes 8000000 | tf_op jit(solution)/shard_map/fused_step/pallas_call | solution.py:298
  135.0 0.6 copy.13
  135.6 0.6 copy.14
  136.3 0.6 copy.15
  136.9 1.3 copy.16
Async XLA Ops:
  0.6 0.9 copy-start
  1.5 0.9 copy-start.1
  2.5 0.9 copy-start.2
  3.4 0.9 copy-start.3
  4.3 0.9 copy-start.4

commit v2 on v0

v2 whole, which is shorter than its diff:
```python
import functools

import jax
import jax.numpy as jnp
from jax import lax
from jax.experimental import pallas as pl
from jax.experimental.pallas import tpu as pltpu
from jax.sharding import PartitionSpec as P

beta_one = 0.9
beta_two = 0.95
learn_rate = 0.0003
decay_rate = 0.1
eps_small = 1e-08
corr_one = 1.0 - 0.9**40
corr_two = 1.0 - 0.95**40

MESH = pl.DeviceIdType.MESH
f32 = jnp.float32
bf16 = jnp.bfloat16
N_COPIES = 96


def kernel(
    stop,
    inputs_hbm, upstream_hbm, master_hbm, moment_one_hbm, moment_two_hbm,
    master_out, first_out, second_out, weights_out,
    feats, state, fresh_state, wown, wbuf, quarter, rs_half, rs_full, dcat,
    featT, gbuf, gy_half, gy_full, gline, gz_in, gin, fin, rows_new,
    send_sems, recv_sems, load_sems, store_sems,
):
    i, j = lax.axis_index("dp"), lax.axis_index("mp")
    z, y, x = i // 16, (i // 4) % 4, i % 4
    zh, core = j // 2, j % 2

    def dev(zh=zh, core=core, z=z, y=y, x=x):
        return (z * 16 + y * 4 + x, zh * 2 + core)

    flip = lambda v: v + 1 - 2 * (v % 2)
    xu, xd, x2 = (x + 1) % 4, (x + 3) % 4, (x + 2) % 4
    yu, yd, y2 = (y + 1) % 4, (y + 3) % 4, (y + 2) % 4
    zu, zd, z2 = (zh + 1) % 4, (zh + 3) % 4, (zh + 2) % 4
    right, left, up, down = dev(x=xu), dev(x=xd), dev(y=yu), dev(y=yd)
    line = [dev(z=(z + k) % 4) for k in (1, 2, 3)]
    skew = [dev(z=(z + k) % 4, x=(x + k) % 4) for k in (1, 2, 3)]
    above, below = dev(zh=zu), dev(zh=zd)
    mate = dev(core=1 - core)
    holder = dev(zh=z, z=x, y=flip(y), x=(zh + x) % 4)
    owner = dev(zh=(x + 4 - z) % 4, z=zh, y=flip(y), x=z)

    started = []

    def put(src, dst, to):
        k = len(started)
        copy = pltpu.make_async_remote_copy(
            src_ref=src, dst_ref=dst, send_sem=send_sems.at[k], recv_sem=recv_sems.at[k],
            device_id=to, device_id_type=MESH,
        )
        copy.start()
        started.append(copy)
        return copy

    def share(ref, to):
        return put(ref, ref, to)

    def arrived(*copies):
        for copy in copies:
            copy.wait_recv()

    def finish():
        for copy in started:
            copy.wait_send()

    barrier = pltpu.get_barrier_semaphore()
    greeted = [right, left, up, down, *line, *skew, above, below, mate, holder, owner]
    for other in greeted:
        pl.semaphore_signal(barrier, inc=1, device_id=other, device_id_type=MESH)

    loads = [
        pltpu.make_async_copy(src, dst, load_sems.at[k])
        for k, (src, dst) in enumerate([
            (master_hbm, state.at[0]),
            (inputs_hbm, feats.at[0, 0, core]),
            (upstream_hbm, feats.at[1, 0, core]),
            (moment_one_hbm, state.at[1]),
            (moment_two_hbm, state.at[2]),
        ])
    ]
    for load in loads:
        load.start()

    def low_lanes(n):
        return lax.broadcasted_iota(jnp.int32, (n, 128), 1) < 64

    def shard_block(rows):
        down_cols = jnp.concatenate([rows[128:192], jnp.zeros((64, 80), f32)], axis=0).T
        rest = jnp.concatenate([down_cols[48:80], jnp.zeros((16, 128), f32)], axis=0)
        folded = down_cols[0:48] + pltpu.roll(rest, 64, 1)
        return jnp.concatenate([rows[0:128].T, folded], axis=0).astype(bf16)

    loads[0].wait()
    wown[...] = shard_block(state[0].reshape(192, 80))
    for load in loads[1:]:
        load.wait()

    pl.semaphore_wait(barrier, len(greeted))

    c_w = put(wown, wbuf.at[y, x], holder)
    own = [feats.at[n, 0, core] for n in (0, 1)]
    c_r = [put(own[n], feats.at[n, 3, core], right) for n in (0, 1)]
    c_l = [put(own[n], feats.at[n, 1, core], left) for n in (1, 0)]
    c_m = [share(own[n], mate) for n in (0, 1)]
    arrived(c_w)
    if stop == 1:
        arrived(*c_r, *c_l, *c_m)
        return finish()
    mine = wbuf.at[flip(y), z]
    c_z = [share(mine, to) for to in skew]
    arrived(c_r[0])
    c_r2 = put(feats.at[0, 3, core], feats.at[0, 2, core], right)
    c_m.append(share(feats.at[0, 3, core], mate))
    arrived(c_l[0])
    c_l2 = put(feats.at[1, 1, core], feats.at[1, 2, core], left)
    c_m.append(share(feats.at[1, 1, core], mate))
    arrived(*c_z)
    if stop == 2:
        arrived(c_r[1], c_l[1], c_r2, c_l2, *c_m)
        return finish()
    mine = wbuf.at[flip(y)]
    c_u, c_d = share(mine, up), share(mine, down)
    arrived(c_r[1])
    c_m.append(share(feats.at[1, 3, core], mate))
    arrived(c_l[1])
    c_m.append(share(feats.at[0, 1, core], mate))
    arrived(c_u)
    c_u2 = share(wbuf.at[flip(yd), pl.ds(0, 2)], up)
    arrived(c_d)
    c_d2 = share(wbuf.at[flip(yu), pl.ds(2, 2)], down)
    arrived(c_r2)
    c_m.append(share(feats.at[0, 2, core], mate))
    arrived(c_l2)
    c_m.append(share(feats.at[1, 2, core], mate))
    arrived(*c_m, c_u2, c_d2)
    if stop == 3:
        return finish()

    w01 = wbuf[:, :, 0:80, :].reshape(1280, 128)
    folded = wbuf[:, :, 80:128, :].reshape(768, 128).astype(f32)
    low = low_lanes(768)
    first_rows = jnp.where(low, folded, 0.0).astype(bf16).reshape(16, 48, 128)
    last_rows = jnp.where(low, pltpu.roll(folded, 64, 1), 0.0).astype(bf16).reshape(16, 48, 128)
    w2 = jnp.concatenate([first_rows, last_rows[:, 0:32]], axis=1).reshape(1280, 128)
    w01 = (w01[0:640], w01[640:1280])
    w2 = (w2[0:640], w2[640:1280])

    def forward(q):
        p01 = jnp.dot(feats[0, q, 0], w01[0], preferred_element_type=f32)
        p01 += jnp.dot(feats[0, q, 1], w01[1], preferred_element_type=f32)
        p2 = jnp.dot(feats[1, q, 0], w2[0], preferred_element_type=f32)
        p2 += jnp.dot(feats[1, q, 1], w2[1], preferred_element_type=f32)
        quarter[q, 0:128] = p01
        quarter[q, 128:192] = p2[0:64] + pltpu.roll(p2[64:128], 64, 1)

    lo, hi = pl.ds(0, 96), pl.ds(96, 96)
    forward(z2)
    c_a1 = put(quarter.at[z2, lo], rs_half.at[0], above)
    c_b1 = put(quarter.at[z2, hi], rs_half.at[1], below)
    forward(zu)
    c_a2 = put(quarter.at[zu, hi], rs_full.at[0, hi], above)
    forward(zd)
    c_b2 = put(quarter.at[zd, lo], rs_full.at[1, lo], below)
    forward(zh)
    arrived(c_a1)
    quarter[zu, 0:96] += rs_half[0]
    c_a3 = put(quarter.at[zu, lo], rs_full.at[0, lo], above)
    arrived(c_b1)
    quarter[zd, 96:192] += rs_half[1]
    c_b3 = put(quarter.at[zd, hi], rs_full.at[1, hi], below)
    for n in (0, 1):
        for q in range(4):
            for d in (0, 1):
                block = feats[n, q, d].T.reshape(2, 320, 128)
                featT[n, 2 * d : 2 * d + 2, :, 128 * q : 128 * q + 128] = block
    arrived(c_a2, c_b2, c_a3, c_b3)
    if stop == 4:
        return finish()

    total = quarter[zh] + rs_full[0] + rs_full[1]
    gate = total[0:128]
    upval = pltpu.roll(gate, 64, 1)
    dhidden = jnp.concatenate([total[128:192], pltpu.roll(total[128:192], 64, 1)], axis=0)
    sigma = jax.nn.sigmoid(gate)
    hidden = gate * sigma * upval
    dgate = dhidden * upval * sigma * (1.0 + gate * (1.0 - sigma))
    dup = dhidden * gate * sigma
    low = low_lanes(128)
    dcat[zh, 0:128] = jnp.where(low, dgate, pltpu.roll(dup, 64, 1)).astype(bf16)
    hidden = jnp.where(low[0:64], hidden[0:64], pltpu.roll(hidden[64:128], 64, 1))
    dcat[zh, 128:192] = hidden.astype(bf16)

    c_a1, c_b1 = share(dcat.at[zh, lo], above), share(dcat.at[zh, hi], below)
    c_a2, c_b2 = share(dcat.at[zh, hi], above), share(dcat.at[zh, lo], below)
    arrived(c_a1)
    c_a3 = share(dcat.at[zd, lo], above)
    arrived(c_b1)
    c_b3 = share(dcat.at[zu, hi], below)
    arrived(c_a2, c_b2, c_a3, c_b3)
    if stop == 5:
        return finish()

    d01 = dcat[:, 0:128, :].reshape(512, 128)
    low = low_lanes(256)
    folded = dcat[:, 128:192, :].reshape(256, 128).astype(f32)
    early = jnp.where(low, folded, 0.0).astype(bf16).reshape(4, 64, 128)
    late = jnp.where(low, pltpu.roll(folded, 64, 1), 0.0).astype(bf16).reshape(4, 64, 128)
    d2 = jnp.concatenate([early, late], axis=1).reshape(512, 128)

    def backward(v):
        p01 = jnp.dot(featT[0, v], d01, preferred_element_type=f32)
        p2 = jnp.dot(featT[1, v], d2, preferred_element_type=f32).reshape(4, 80, 128)
        rest = pltpu.roll(p2[:, 40:80].reshape(160, 128), 64, 1).reshape(4, 40, 128)
        gbuf[v, :, 0:80] = p01.reshape(4, 80, 128)
        gbuf[v, :, 80:120] = p2[:, 0:40] + rest

    lo, hi = pl.ds(0, 2), pl.ds(2, 2)
    backward(flip(y2))
    c_a1 = put(gbuf.at[flip(y2), lo], gy_half.at[0], up)
    c_b1 = put(gbuf.at[flip(y2), hi], gy_half.at[1], down)
    backward(flip(yu))
    c_a2 = put(gbuf.at[flip(yu), hi], gy_full.at[0, hi], up)
    backward(flip(yd))
    c_b2 = put(gbuf.at[flip(yd), lo], gy_full.at[1, lo], down)
    backward(flip(y))
    arrived(c_a1)
    gbuf[flip(yu), 0:2] += gy_half[0]
    c_a3 = put(gbuf.at[flip(yu), lo], gy_full.at[0, lo], up)
    arrived(c_b1)
    gbuf[flip(yd), 2:4] += gy_half[1]
    c_b3 = put(gbuf.at[flip(yd), hi], gy_full.at[1, hi], down)
    arrived(c_a2, c_b2, c_a3, c_b3)
    gline[...] = gbuf[flip(y)] + gy_full[0] + gy_full[1]
    if stop == 6:
        return finish()
    c_z = [put(gline.at[(z + k) % 4], gz_in.at[k - 1], skew[k - 1]) for k in (1, 2, 3)]
    arrived(*c_z)
    gline[z] += gz_in[0] + gz_in[1] + gz_in[2]
    if stop == 7:
        return finish()

    arrived(put(gline.at[z], gin, owner))
    if stop == 8:
        return finish()

    g01 = gin[0:80]
    g2 = jnp.concatenate([gin[80:120], pltpu.roll(gin[80:120], 64, 1)], axis=0)
    grads = jnp.concatenate([g01.T, g2.T[0:64]], axis=0).reshape(3, 64, 80)
    master, moment_one, moment_two = state[0], state[1], state[2]
    first = beta_one * moment_one + (1.0 - beta_one) * grads
    second = beta_two * moment_two + (1.0 - beta_two) * grads * grads
    update = first / corr_one / (jnp.sqrt(second / corr_two) + eps_small)
    fresh = master - learn_rate * (update + decay_rate * master)
    fin[y, x, z] = shard_block(fresh.reshape(192, 80))

    c_z = [share(fin.at[y, x, z], to) for to in line]
    fresh_state[0] = fresh
    fresh_state[1] = first
    fresh_state[2] = second
    stores = [
        pltpu.make_async_copy(fresh_state.at[k], out, store_sems.at[k])
        for k, out in enumerate((master_out, first_out, second_out))
    ]
    for store in stores:
        store.start()
    arrived(*c_z)
    if stop == 9:
        for store in stores:
            store.wait()
        return finish()

    mine = fin.at[y, x]
    c_r, c_l, c_u, c_d = (share(mine, to) for to in (right, left, up, down))
    a, b = pl.ds(0, 2), pl.ds(2, 2)
    part = lambda yy, xx, s: fin.at[yy, xx, s]
    arrived(c_r)
    c_ax = [share(part(y, xd, 0), right)]
    ay1 = [share(part(y, xd, a), up), share(part(y, xd, a), down)]
    arrived(c_l)
    c_ax.append(share(part(y, xu, 1), left))
    ay2 = [share(part(y, xu, a), up), share(part(y, xu, a), down)]
    arrived(c_u)
    c_by = [share(part(yd, x, 2), up)]
    bx1 = [share(part(yd, x, b), right), share(part(yd, x, b), left)]
    arrived(c_d)
    c_by.append(share(part(yu, x, 3), down))
    bx2 = [share(part(yu, x, b), right), share(part(yu, x, b), left)]
    last = [
        share(part(yd, x, 0), up), share(part(yu, x, 1), down),
        share(part(y, xd, 2), right), share(part(y, xu, 3), left),
    ]
    arrived(*c_ax)
    ay3 = [share(part(y, x2, a), up), share(part(y, x2, a), down)]
    arrived(*c_by)
    bx3 = [share(part(y2, x, b), right), share(part(y2, x, b), left)]
    for va, vb, ca, cb in ((xd, yd, ay1, bx1), (xu, yu, ay2, bx2), (x2, y2, ay3, bx3)):
        arrived(ca[0])
        last.append(share(part(yd, va, 0), up))
        arrived(ca[1])
        last.append(share(part(yu, va, 1), down))
        arrived(cb[0])
        last.append(share(part(vb, xd, 2), right))
        arrived(cb[1])
        last.append(share(part(vb, xu, 3), left))
    arrived(*last)
    if stop == 10:
        for store in stores:
            store.wait()
        return finish()

    low = low_lanes(768)
    for n in range(4):
        cols = slice(1280 * n, 1280 * n + 1280)
        both = fin[:, :, n, 0:80, :].reshape(1280, 128).T
        rows_new[0, :, cols] = both[0:64]
        rows_new[1, :, cols] = both[64:128]
        folded = fin[:, :, n, 80:128, :].reshape(768, 128).astype(f32)
        rest = pltpu.roll(folded, 64, 1).reshape(16, 48, 128)[:, 0:32]
        third = jnp.concatenate([folded.reshape(16, 48, 128), rest], axis=1)
        rows_new[2, :, cols] = third.reshape(1280, 128).astype(bf16).T[0:64]
        store = pltpu.make_async_copy(
            rows_new.at[:, :, pl.ds(1280 * n, 1280)],
            weights_out.at[:, :, pl.ds(1280 * n, 1280)],
            store_sems.at[3 + n],
        )
        store.start()
        stores.append(store)
    for store in stores:
        store.wait()
    finish()


def local(stop, inputs, upstream, master, moment_one, moment_two):
    shard = jax.ShapeDtypeStruct((3, 64, 80), f32)
    hbm = pl.BlockSpec(memory_space=pltpu.HBM)
    return pl.pallas_call(
        functools.partial(kernel, stop),
        out_shape=(shard, shard, shard, jax.ShapeDtypeStruct((3, 64, 5120), bf16)),
        in_specs=[hbm] * 5,
        out_specs=(hbm,) * 4,
        scratch_shapes=[
            pltpu.VMEM((2, 4, 2, 128, 640), bf16),
            pltpu.VMEM((3, 3, 64, 80), f32),
            pltpu.VMEM((3, 3, 64, 80), f32),
            pltpu.VMEM((128, 128), bf16),
            pltpu.VMEM((4, 4, 128, 128), bf16),
            pltpu.VMEM((4, 192, 128), f32),
            pltpu.VMEM((2, 96, 128), f32),
            pltpu.VMEM((2, 192, 128), f32),
            pltpu.VMEM((4, 192, 128), bf16),
            pltpu.VMEM((2, 4, 320, 512), bf16),
            pltpu.VMEM((4, 4, 120, 128), f32),
            pltpu.VMEM((2, 2, 120, 128), f32),
            pltpu.VMEM((2, 4, 120, 128), f32),
            pltpu.VMEM((4, 120, 128), f32),
            pltpu.VMEM((3, 120, 128), f32),
            pltpu.VMEM((120, 128), f32),
            pltpu.VMEM((4, 4, 4, 128, 128), bf16),
            pltpu.VMEM((3, 64, 5120), bf16),
            pltpu.SemaphoreType.DMA((N_COPIES,)),
            pltpu.SemaphoreType.DMA((N_COPIES,)),
            pltpu.SemaphoreType.DMA((5,)),
            pltpu.SemaphoreType.DMA((7,)),
        ],
        compiler_params=pltpu.CompilerParams(
            collective_id=0, has_side_effects=True, vmem_limit_bytes=40 * 2**20
        ),
        cost_estimate=pl.CostEstimate(
            flops=503316480, bytes_accessed=8000000, transcendentals=8192
        ),
        name="fused_step",
    )(inputs, upstream, master, moment_one, moment_two)


def solution(mesh, stop=0):
    owned = P(None, "mp", "dp")
    return jax.shard_map(
        functools.partial(local, stop),
        mesh=mesh,
        in_specs=(P("dp", "mp"), P("dp", "mp"), owned, owned, owned),
        out_specs=(owned, owned, owned, P(None, "mp", None)),
        check_vma=False,
    )
```

time: 1260 us -> 122 us (0.10)
  waiting for transfers between devices: 1170 us -> 0 us
  Pallas kernels: 0 us -> 113 us
  local copies, waits for them, and re-layouts: 58.7 us -> 7.69 us
  between operations: 13.9 us -> 0.65 us
    all_gather x4 -> x0, waiting for transfers between devices: 798 us -> none  [the longest x1 365 us: local(): lax.all_gather(master.astype(jnp.bfloat16), 'dp', axis=2, tiled=True)]
    unnamed x6 -> x0, waiting for transfers between devices: 376 us -> none
    pallas_call x0 -> x1, Pallas kernels: none -> 113 us  [local(): pl.pallas_call(functools.partial(kernel, stop), out_shape=(shard, shard,...]
    unnamed x20 -> x14, local copies, waits for them, and re-layouts: 43.9 us -> 7.69 us
    slice x1 -> x0, local copies, waits for them, and re-layouts: 13.3 us -> none  [local(): dhidden = contract_width(cotan_full, piece[2])]
  transfers between devices with their start and end apart: 5 -> 0, of which waited for: 5 -> 0; matrix products, arithmetic and copies ran while one was open for 2% -> 0% of each run, Pallas kernels for 0% -> 0%
where the time goes in v2:
time: 122 us
  Pallas kernels  113 us (93%)
  local copies, waits for them, and re-layouts  7.69 us (6%)
    pallas_call x1, Pallas kernels, local(): pl.pallas_call(functools.partial(kernel, stop), out_shape=(shard, shard,...  113 us
    unnamed x14, local copies, waits for them, and re-layouts  7.69 us

profile of v2, /device:TPU:4, one launch (start us, length us, event | category | flops | bytes accessed | tf_op | source)
XLA Modules:
  0.0 121.8 jit_solution(5434550588224197345)
XLA Ops:
  0.6 0.0 copy-start
  0.6 0.9 copy-done
  1.5 0.0 copy-start.1
  1.6 0.9 copy-done.1
  2.5 0.0 copy-start.2
  2.5 0.9 copy-done.2
  3.4 0.0 copy-start.3
  3.4 0.9 copy-done.3
  4.3 0.0 copy-start.4
  4.3 0.9 copy-done.4
  5.1 113.4 %fused_step.1 = (f32[3,64,80]{2,1,0:T(8,128)S(1)}, f32[3,64,80]{2,1,0:T(8,128)S(1)}, f32[3,64,80]{2,1,0:T(8,128)S(1)}, bf16[3,64,5120]{2,1,0:T(8,128)(2,1)S(1)}) custom-call(bf16[128,640]{1,0:T(8,128)(2,1)S(1)} %copy-done, bf16[128,640]{1,0:T(8,128)(2,1)S(1)} %copy-done.1, f32[3,64,80]{2,1,0:T(8,128)S(1)} %copy-done.2, f32[3,64,80]{2,1,0:T(8,128)S(1)} %copy-done.3, ...), custom_call_target="tpu_custom_call" | custom-call | flops 503316480 | bytes 8000000 | tf_op jit(solution)/shard_map/fused_step/pallas_call | solution.py:344
  118.6 0.6 copy.13
  119.2 0.6 copy.14
  119.9 0.6 copy.15
  120.5 1.3 %copy.16 = bf16[3,64,5120]{2,1,0:T(8,128)(2,1)} copy(bf16[3,64,5120]{2,1,0:T(8,128)(2,1)S(1)} %get-tuple-element.11) | data formatting | bytes 3932160
Async XLA Ops:
  0.6 0.9 copy-start
  1.5 0.9 copy-start.1
  2.5 0.9 copy-start.2
  3.4 0.9 copy-start.3
  4.3 0.9 copy-start.4

commit v3 on v2

--- a/solution.py
+++ b/solution.py
@@ -18,14 +18,21 @@
 MESH = pl.DeviceIdType.MESH
 f32 = jnp.float32
 bf16 = jnp.bfloat16
-N_COPIES = 96
+N_COPIES = 128
+
+
+def adamw(grads, master, moment_one, moment_two):
+    first = beta_one * moment_one + (1.0 - beta_one) * grads
+    second = beta_two * moment_two + (1.0 - beta_two) * grads * grads
+    update = first / corr_one / (jnp.sqrt(second / corr_two) + eps_small)
+    return first, second, master - learn_rate * (update + decay_rate * master)
 
 
 def kernel(
     stop,
     inputs_hbm, upstream_hbm, master_hbm, moment_one_hbm, moment_two_hbm,
-    master_out, first_out, second_out, weights_out,
-    feats, state, fresh_state, wown, wbuf, quarter, rs_half, rs_full, dcat,
+    grads_out, weights_out,
+    feats, state, grads_own, wown, wbuf, quarter, rs_half, rs_full, dcat,
     featT, gbuf, gy_half, gy_full, gline, gz_in, gin, fin, rows_new,
     send_sems, recv_sems, load_sems, store_sems,
 ):
@@ -41,12 +48,17 @@
     yu, yd, y2 = (y + 1) % 4, (y + 3) % 4, (y + 2) % 4
     zu, zd, z2 = (zh + 1) % 4, (zh + 3) % 4, (zh + 2) % 4
     right, left, up, down = dev(x=xu), dev(x=xd), dev(y=yu), dev(y=yd)
+    across_x, across_y = dev(x=x2), dev(y=y2)
     line = [dev(z=(z + k) % 4) for k in (1, 2, 3)]
     skew = [dev(z=(z + k) % 4, x=(x + k) % 4) for k in (1, 2, 3)]
     above, below = dev(zh=zu), dev(zh=zd)
     mate = dev(core=1 - core)
-    holder = dev(zh=z, z=x, y=flip(y), x=(zh + x) % 4)
-    owner = dev(zh=(x + 4 - z) % 4, z=zh, y=flip(y), x=z)
+    holders = [
+        dev(zh=z, z=(x + m) % 4, y=flip(y), x=(zh + x + m) % 4) for m in range(4)
+    ]
+    owners = [
+        dev(zh=(x + 4 - z) % 4, z=zh, y=flip(y), x=(z + 4 - m) % 4) for m in range(4)
+    ]
 
     started = []
 
@@ -72,7 +84,10 @@
             copy.wait_send()
 
     barrier = pltpu.get_barrier_semaphore()
-    greeted = [right, left, up, down, *line, *skew, above, below, mate, holder, owner]
+    greeted = [
+        *holders, *owners, above, below, *line, *skew,
+        right, left, up, down, across_x, across_y, mate,
+    ]
     for other in greeted:
         pl.semaphore_signal(barrier, inc=1, device_id=other, device_id_type=MESH)
 
@@ -105,42 +120,44 @@
 
     pl.semaphore_wait(barrier, len(greeted))
 
-    c_w = put(wown, wbuf.at[y, x], holder)
+    c_w = [put(wown, wbuf.at[y, x], to) for to in holders]
     own = [feats.at[n, 0, core] for n in (0, 1)]
     c_r = [put(own[n], feats.at[n, 3, core], right) for n in (0, 1)]
     c_l = [put(own[n], feats.at[n, 1, core], left) for n in (1, 0)]
     c_m = [share(own[n], mate) for n in (0, 1)]
-    arrived(c_w)
-    if stop == 1:
-        arrived(*c_r, *c_l, *c_m)
-        return finish()
-    mine = wbuf.at[flip(y), z]
-    c_z = [share(mine, to) for to in skew]
+    c_y = []
+
+    def spread(m):
+        arrived(c_w[m])
+        piece = wbuf.at[flip(y), (z + 4 - m) % 4]
+        c_y.extend(share(piece, to) for to in (up, down, across_y))
+
+    spread(0)
+    spread(1)
     arrived(c_r[0])
     c_r2 = put(feats.at[0, 3, core], feats.at[0, 2, core], right)
-    c_m.append(share(feats.at[0, 3, core], mate))
     arrived(c_l[0])
     c_l2 = put(feats.at[1, 1, core], feats.at[1, 2, core], left)
+    spread(2)
+    spread(3)
+    if stop == 1:
+        arrived(*c_y, c_r[1], c_l[1], c_r2, c_l2, *c_m)
+        return finish()
+    c_m.append(share(feats.at[0, 3, core], mate))
     c_m.append(share(feats.at[1, 1, core], mate))
-    arrived(*c_z)
-    if stop == 2:
-        arrived(c_r[1], c_l[1], c_r2, c_l2, *c_m)
-        return finish()
-    mine = wbuf.at[flip(y)]
-    c_u, c_d = share(mine, up), share(mine, down)
     arrived(c_r[1])
     c_m.append(share(feats.at[1, 3, core], mate))
     arrived(c_l[1])
     c_m.append(share(feats.at[0, 1, core], mate))
-    arrived(c_u)
-    c_u2 = share(wbuf.at[flip(yd), pl.ds(0, 2)], up)
-    arrived(c_d)
-    c_d2 = share(wbuf.at[flip(yu), pl.ds(2, 2)], down)
     arrived(c_r2)
     c_m.append(share(feats.at[0, 2, core], mate))
     arrived(c_l2)
     c_m.append(share(feats.at[1, 2, core], mate))
-    arrived(*c_m, c_u2, c_d2)
+    arrived(*c_y)
+    if stop == 2:
+        arrived(*c_m)
+        return finish()
+    arrived(*c_m)
     if stop == 3:
         return finish()
 
@@ -247,92 +264,110 @@
     if stop == 7:
         return finish()
 
-    arrived(put(gline.at[z], gin, owner))
+    arrived(put(gline.at[z], gin, owners[0]))
     if stop == 8:
         return finish()
 
     g01 = gin[0:80]
     g2 = jnp.concatenate([gin[80:120], pltpu.roll(gin[80:120], 64, 1)], axis=0)
     grads = jnp.concatenate([g01.T, g2.T[0:64]], axis=0).reshape(3, 64, 80)
-    master, moment_one, moment_two = state[0], state[1], state[2]
-    first = beta_one * moment_one + (1.0 - beta_one) * grads
-    second = beta_two * moment_two + (1.0 - beta_two) * grads * grads
-    update = first / corr_one / (jnp.sqrt(second / corr_two) + eps_small)
-    fresh = master - learn_rate * (update + decay_rate * master)
-    fin[y, x, z] = shard_block(fresh.reshape(192, 80))
-
-    c_z = [share(fin.at[y, x, z], to) for to in line]
-    fresh_state[0] = fresh
-    fresh_state[1] = first
-    fresh_state[2] = second
-    stores = [
-        pltpu.make_async_copy(fresh_state.at[k], out, store_sems.at[k])
-        for k, out in enumerate((master_out, first_out, second_out))
-    ]
-    for store in stores:
+    fresh = adamw(grads, state[0], state[1], state[2])[2]
+    fin[y, x, 0] = shard_block(fresh.reshape(192, 80))
+
+    c_z = [put(fin.at[y, x, 0], fin.at[y, x, 4 - k], line[k - 1]) for k in (1, 2, 3)]
+    grads_own[...] = grads
+    stores = [pltpu.make_async_copy(grads_own, grads_out, store_sems.at[0])]
+    stores[0].start()
+
+    class Plane:
+        def __init__(self, slots):
+            self.slots = slots
+
+        def at(self, yy, xx, start=0, size=128):
+            return fin.at[yy, xx, self.slots, pl.ds(start, size)]
+
+        def begin(self):
+            mine = self.at(y, x)
+            self.r, self.l, self.u, self.d = (share(mine, to) for to in (right, left, up, down))
+            self.x2 = share(self.at(y, x, 0, 64), across_x)
+            self.y2 = share(self.at(y, x, 64, 64), across_y)
+
+        def turn(self):
+            def columns(xx):
+                return [share(self.at(y, xx, 0, 64), to) for to in (up, down)]
+
+            def rows(yy):
+                return [share(self.at(yy, x, 64, 64), to) for to in (right, left)]
+
+            arrived(self.r)
+            self.a = [columns(xd)]
+            self.last = [share(self.at(y, xd, 64, 32), right)]
+            arrived(self.u)
+            self.b = [rows(yd)]
+            self.last.append(share(self.at(yd, x, 0, 32), up))
+            arrived(self.l)
+            self.a.append(columns(xu))
+            self.last.append(share(self.at(y, xu, 96, 32), left))
+            arrived(self.d)
+            self.b.append(rows(yu))
+            self.last.append(share(self.at(yu, x, 32, 32), down))
+            arrived(self.x2)
+            self.a.append(columns(x2))
+            arrived(self.y2)
+            self.b.append(rows(y2))
+
+        def forward(self):
+            for xx, yy, a, b in zip((xd, xu, x2), (yd, yu, y2), self.a, self.b):
+                arrived(a[0])
+                self.last.append(share(self.at(yd, xx, 0, 32), up))
+                arrived(b[0])
+                self.last.append(share(self.at(yy, xd, 64, 32), right))
+                arrived(a[1])
+                self.last.append(share(self.at(yu, xx, 32, 32), down))
+                arrived(b[1])
+                self.last.append(share(self.at(yy, xu, 96, 32), left))
+
+        def end(self):
+            arrived(*self.last)
+
+    def unpack(r):
+        n = (z + r) % 4
+        both = fin[:, :, r, 0:80, :].reshape(1280, 128).T
+        rows_new[n, 0] = both[0:64]
+        rows_new[n, 1] = both[64:128]
+        folded = fin[:, :, r, 80:128, :].reshape(768, 128).astype(f32)
+        rest = pltpu.roll(folded, 64, 1).reshape(16, 48, 128)[:, 0:32]
+        third = jnp.concatenate([folded.reshape(16, 48, 128), rest], axis=1)
+        rows_new[n, 2] = third.reshape(1280, 128).astype(bf16).T[0:64]
+        columns = pl.ds(pl.multiple_of(n * 1280, 128), 1280)
+        store = pltpu.make_async_copy(
+            rows_new.at[n], weights_out.at[:, :, columns], store_sems.at[1 + r]
+        )
         store.start()
+        stores.append(store)
+
+    near, far = Plane(pl.ds(0, 1)), Plane(pl.ds(1, 3))
+    near.begin()
+    near.turn()
     arrived(*c_z)
     if stop == 9:
-        for store in stores:
-            store.wait()
-        return finish()
-
-    mine = fin.at[y, x]
-    c_r, c_l, c_u, c_d = (share(mine, to) for to in (right, left, up, down))
-    a, b = pl.ds(0, 2), pl.ds(2, 2)
-    part = lambda yy, xx, s: fin.at[yy, xx, s]
-    arrived(c_r)
-    c_ax = [share(part(y, xd, 0), right)]
-    ay1 = [share(part(y, xd, a), up), share(part(y, xd, a), down)]
-    arrived(c_l)
-    c_ax.append(share(part(y, xu, 1), left))
-    ay2 = [share(part(y, xu, a), up), share(part(y, xu, a), down)]
-    arrived(c_u)
-    c_by = [share(part(yd, x, 2), up)]
-    bx1 = [share(part(yd, x, b), right), share(part(yd, x, b), left)]
-    arrived(c_d)
-    c_by.append(share(part(yu, x, 3), down))
-    bx2 = [share(part(yu, x, b), right), share(part(yu, x, b), left)]
-    last = [
-        share(part(yd, x, 0), up), share(part(yu, x, 1), down),
-        share(part(y, xd, 2), right), share(part(y, xu, 3), left),
-    ]
-    arrived(*c_ax)
-    ay3 = [share(part(y, x2, a), up), share(part(y, x2, a), down)]
-    arrived(*c_by)
-    bx3 = [share(part(y2, x, b), right), share(part(y2, x, b), left)]
-    for va, vb, ca, cb in ((xd, yd, ay1, bx1), (xu, yu, ay2, bx2), (x2, y2, ay3, bx3)):
-        arrived(ca[0])
-        last.append(share(part(yd, va, 0), up))
-        arrived(ca[1])
-        last.append(share(part(yu, va, 1), down))
-        arrived(cb[0])
-        last.append(share(part(vb, xd, 2), right))
-        arrived(cb[1])
-        last.append(share(part(vb, xu, 3), left))
-    arrived(*last)
+        near.forward()
+        near.end()
+        stores[0].wait()
+        return finish()
+    far.begin()
+    near.forward()
+    far.turn()
+    near.end()
+    unpack(0)
+    far.forward()
+    far.end()
     if stop == 10:
         for store in stores:
             store.wait()
         return finish()
-
-    low = low_lanes(768)
-    for n in range(4):
-        cols = slice(1280 * n, 1280 * n + 1280)
-        both = fin[:, :, n, 0:80, :].reshape(1280, 128).T
-        rows_new[0, :, cols] = both[0:64]
-        rows_new[1, :, cols] = both[64:128]
-        folded = fin[:, :, n, 80:128, :].reshape(768, 128).astype(f32)
-        rest = pltpu.roll(folded, 64, 1).reshape(16, 48, 128)[:, 0:32]
-        third = jnp.concatenate([folded.reshape(16, 48, 128), rest], axis=1)
-        rows_new[2, :, cols] = third.reshape(1280, 128).astype(bf16).T[0:64]
-        store = pltpu.make_async_copy(
-            rows_new.at[:, :, pl.ds(1280 * n, 1280)],
-            weights_out.at[:, :, pl.ds(1280 * n, 1280)],
-            store_sems.at[3 + n],
-        )
-        store.start()
-        stores.append(store)
+    for r in (1, 2, 3):
+        unpack(r)
     for store in stores:
         store.wait()
     finish()
@@ -341,15 +376,15 @@
 def local(stop, inputs, upstream, master, moment_one, moment_two):
     shard = jax.ShapeDtypeStruct((3, 64, 80), f32)
     hbm = pl.BlockSpec(memory_space=pltpu.HBM)
-    return pl.pallas_call(
+    grads, weights = pl.pallas_call(
         functools.partial(kernel, stop),
-        out_shape=(shard, shard, shard, jax.ShapeDtypeStruct((3, 64, 5120), bf16)),
+        out_shape=(shard, jax.ShapeDtypeStruct((3, 64, 5120), bf16)),
         in_specs=[hbm] * 5,
-        out_specs=(hbm,) * 4,
+        out_specs=(hbm,) * 2,
         scratch_shapes=[
             pltpu.VMEM((2, 4, 2, 128, 640), bf16),
             pltpu.VMEM((3, 3, 64, 80), f32),
-            pltpu.VMEM((3, 3, 64, 80), f32),
+            pltpu.VMEM((3, 64, 80), f32),
             pltpu.VMEM((128, 128), bf16),
             pltpu.VMEM((4, 4, 128, 128), bf16),
             pltpu.VMEM((4, 192, 128), f32),
@@ -364,20 +399,22 @@
             pltpu.VMEM((3, 120, 128), f32),
             pltpu.VMEM((120, 128), f32),
             pltpu.VMEM((4, 4, 4, 128, 128), bf16),
-            pltpu.VMEM((3, 64, 5120), bf16),
+            pltpu.VMEM((4, 3, 64, 1280), bf16),
             pltpu.SemaphoreType.DMA((N_COPIES,)),
             pltpu.SemaphoreType.DMA((N_COPIES,)),
             pltpu.SemaphoreType.DMA((5,)),
-            pltpu.SemaphoreType.DMA((7,)),
+            pltpu.SemaphoreType.DMA((5,)),
         ],
         compiler_params=pltpu.CompilerParams(
-            collective_id=0, has_side_effects=True, vmem_limit_bytes=40 * 2**20
+            collective_id=0, has_side_effects=True, vmem_limit_bytes=62 * 2**20
         ),
         cost_estimate=pl.CostEstimate(
             flops=503316480, bytes_accessed=8000000, transcendentals=8192
         ),
         name="fused_step",
     )(inputs, upstream, master, moment_one, moment_two)
+    first, second, fresh = adamw(grads, master, moment_one, moment_two)
+    return fresh, first, second, weights
 
 
 def solution(mesh, stop=0):

time: 122 us -> 115 us (0.943)
  the two profiles are of different devices: /device:TPU:4 before, /device:TPU:64 now
where the time goes in v3:
time: 115 us
  Pallas kernels  110 us (96%)
  local copies, waits for them, and re-layouts  2.94 us (3%)
  other arithmetic  1.78 us (2%)
    pallas_call x1, Pallas kernels, local(): pl.pallas_call(functools.partial(kernel, stop), out_shape=(shard, jax.Sha...  110 us
    unnamed x1, local copies, waits for them, and re-layouts  2.94 us

profile of v3, /device:TPU:64, one launch (start us, length us, event | category | flops | bytes accessed | tf_op | source)
XLA Modules:
  0.0 115.3 jit_solution(16349994077342455629)
XLA Ops:
  0.6 109.9 %fused_step.1 = (f32[3,64,80]{2,1,0:T(8,128)}, bf16[3,64,5120]{2,1,0:T(8,128)(2,1)}) custom-call(bf16[128,640]{1,0:T(8,128)(2,1)} %inputs_hbm.1, bf16[128,640]{1,0:T(8,128)(2,1)} %upstream_hbm.1, f32[3,64,80]{2,1,0:T(8,128)} %master_hbm.1, f32[3,64,80]{2,1,0:T(8,128)} %moment_one_hbm.1, f32[3,64,80]{2,1,0:T(8,128)} %moment_two_hbm.1), custom_call_target="tpu_custom_call" | custom-call | flops 503316480 | bytes 8000000 | tf_op jit(solution)/shard_map/fused_step/pallas_call | solution.py:379
  110.5 1.8 %multiply_subtract_fusion = (f32[3,64,80]{2,1,0:T(8,128)}, f32[3,64,80]{2,1,0:T(8,128)}, f32[3,64,80]{2,1,0:T(8,128)}) fusion(f32[3,64,80]{2,1,0:T(8,128)} %master_hbm.1, f32[3,64,80]{2,1,0:T(8,128)} %get-tuple-element.6, f32[3,64,80]{2,1,0:T(8,128)} %moment_one_hbm.1, f32[3,64,80]{2,1,0:T(8,128)} %moment_two_hbm.1), kind=kLoop, calls=%fused_computation.2 | loop fusion | flops 230400 | bytes 430080 | tf_op jit(solution)/shard_map/sub | solution.py:28
  112.3 2.9 %copy.10 = bf16[3,64,5120]{2,1,0:T(8,128)(2,1)} copy(bf16[3,64,5120]{2,1,0:T(8,128)(2,1)} %get-tuple-element.18) | data formatting | bytes 3932160

commit v4 on v3

--- a/solution.py
+++ b/solution.py
@@ -18,7 +18,7 @@
 MESH = pl.DeviceIdType.MESH
 f32 = jnp.float32
 bf16 = jnp.bfloat16
-N_COPIES = 128
+N_COPIES = 160
 
 
 def adamw(grads, master, moment_one, moment_two):
@@ -52,7 +52,7 @@
     line = [dev(z=(z + k) % 4) for k in (1, 2, 3)]
     skew = [dev(z=(z + k) % 4, x=(x + k) % 4) for k in (1, 2, 3)]
     above, below = dev(zh=zu), dev(zh=zd)
-    mate = dev(core=1 - core)
+    opposed, mate = dev(zh=z2), dev(core=1 - core)
     holders = [
         dev(zh=z, z=(x + m) % 4, y=flip(y), x=(zh + x + m) % 4) for m in range(4)
     ]
@@ -85,7 +85,7 @@
 
     barrier = pltpu.get_barrier_semaphore()
     greeted = [
-        *holders, *owners, above, below, *line, *skew,
+        *holders, *owners, above, below, opposed, *line, *skew,
         right, left, up, down, across_x, across_y, mate,
     ]
     for other in greeted:
@@ -120,85 +120,111 @@
 
     pl.semaphore_wait(barrier, len(greeted))
 
-    c_w = [put(wown, wbuf.at[y, x], to) for to in holders]
+    gate_up, down_part = pl.ds(0, 80), pl.ds(80, 48)
+    c_w = [
+        [put(wown.at[rows], wbuf.at[y, x, rows], to) for to in holders]
+        for rows in (gate_up, down_part)
+    ]
     own = [feats.at[n, 0, core] for n in (0, 1)]
-    c_r = [put(own[n], feats.at[n, 3, core], right) for n in (0, 1)]
-    c_l = [put(own[n], feats.at[n, 1, core], left) for n in (1, 0)]
-    c_m = [share(own[n], mate) for n in (0, 1)]
-    c_y = []
-
-    def spread(m):
-        arrived(c_w[m])
-        piece = wbuf.at[flip(y), (z + 4 - m) % 4]
-        c_y.extend(share(piece, to) for to in (up, down, across_y))
-
-    spread(0)
-    spread(1)
+    c_r, c_l = [], []
+    for n in (0, 1):
+        c_r.append(put(own[n], feats.at[n, 3, core], right))
+        c_l.append(put(own[n], feats.at[n, 1, core], left))
+    c_m = [[share(own[n], mate)] for n in (0, 1)]
+    c_y = [[], []]
+
+    def spread(n, m):
+        arrived(c_w[n][m])
+        piece = wbuf.at[flip(y), (z + 4 - m) % 4, (gate_up, down_part)[n]]
+        c_y[n].extend(share(piece, to) for to in (up, down, across_y))
+
+    spread(0, 0)
+    spread(0, 1)
     arrived(c_r[0])
     c_r2 = put(feats.at[0, 3, core], feats.at[0, 2, core], right)
+    c_m[0].append(share(feats.at[0, 3, core], mate))
+    spread(0, 2)
+    spread(0, 3)
     arrived(c_l[0])
+    c_m[0].append(share(feats.at[0, 1, core], mate))
+    arrived(c_l[1])
     c_l2 = put(feats.at[1, 1, core], feats.at[1, 2, core], left)
-    spread(2)
-    spread(3)
+    c_m[1].append(share(feats.at[1, 1, core], mate))
+    for m in range(4):
+        spread(1, m)
+    arrived(c_r[1])
+    c_m[1].append(share(feats.at[1, 3, core], mate))
+    arrived(c_r2)
+    c_m[0].append(share(feats.at[0, 2, core], mate))
+    arrived(c_l2)
+    c_m[1].append(share(feats.at[1, 2, core], mate))
+    arrived(*c_m[0], *c_y[0])
     if stop == 1:
-        arrived(*c_y, c_r[1], c_l[1], c_r2, c_l2, *c_m)
-        return finish()
-    c_m.append(share(feats.at[0, 3, core], mate))
-    c_m.append(share(feats.at[1, 1, core], mate))
-    arrived(c_r[1])
-    c_m.append(share(feats.at[1, 3, core], mate))
-    arrived(c_l[1])
-    c_m.append(share(feats.at[0, 1, core], mate))
-    arrived(c_r2)
-    c_m.append(share(feats.at[0, 2, core], mate))
-    arrived(c_l2)
-    c_m.append(share(feats.at[1, 2, core], mate))
-    arrived(*c_y)
-    if stop == 2:
-        arrived(*c_m)
-        return finish()
-    arrived(*c_m)
-    if stop == 3:
+        arrived(*c_m[1], *c_y[1])
         return finish()
 
     w01 = wbuf[:, :, 0:80, :].reshape(1280, 128)
+    w01 = (w01[0:640], w01[640:1280])
+
+    def forward01(q):
+        p01 = jnp.dot(feats[0, q, 0], w01[0], preferred_element_type=f32)
+        p01 += jnp.dot(feats[0, q, 1], w01[1], preferred_element_type=f32)
+        quarter[q, 0:128] = p01
+
+    def forward2(q):
+        p2 = jnp.dot(feats[1, q, 0], w2[0], preferred_element_type=f32)
+        p2 += jnp.dot(feats[1, q, 1], w2[1], preferred_element_type=f32)
+        quarter[q, 128:192] = p2[0:64] + pltpu.roll(p2[64:128], 64, 1)
+
+    lo, hi = (pl.ds(0, 64), pl.ds(128, 32)), (pl.ds(64, 64), pl.ds(160, 32))
+
+    def opposite(n):
+        return (
+            put(quarter.at[z2, lo[n]], rs_half.at[lo[n]], above),
+            put(quarter.at[z2, hi[n]], rs_half.at[hi[n]], below),
+        )
+
+    def direct(n):
+        return (
+            put(quarter.at[zu, hi[n]], rs_full.at[0, hi[n]], above),
+            put(quarter.at[zd, lo[n]], rs_full.at[1, lo[n]], below),
+        )
+
+    def onward(n, c_a, c_b):
+        arrived(c_a)
+        quarter[zu, lo[n]] += rs_half[lo[n]]
+        c_up = put(quarter.at[zu, lo[n]], rs_full.at[0, lo[n]], above)
+        arrived(c_b)
+        quarter[zd, hi[n]] += rs_half[hi[n]]
+        return c_up, put(quarter.at[zd, hi[n]], rs_full.at[1, hi[n]], below)
+
+    forward01(z2)
+    c_o1 = opposite(0)
+    forward01(zu)
+    forward01(zd)
+    arrived(*c_m[1], *c_y[1])
     folded = wbuf[:, :, 80:128, :].reshape(768, 128).astype(f32)
     low = low_lanes(768)
     first_rows = jnp.where(low, folded, 0.0).astype(bf16).reshape(16, 48, 128)
     last_rows = jnp.where(low, pltpu.roll(folded, 64, 1), 0.0).astype(bf16).reshape(16, 48, 128)
     w2 = jnp.concatenate([first_rows, last_rows[:, 0:32]], axis=1).reshape(1280, 128)
-    w01 = (w01[0:640], w01[640:1280])
     w2 = (w2[0:640], w2[640:1280])
-
-    def forward(q):
-        p01 = jnp.dot(feats[0, q, 0], w01[0], preferred_element_type=f32)
-        p01 += jnp.dot(feats[0, q, 1], w01[1], preferred_element_type=f32)
-        p2 = jnp.dot(feats[1, q, 0], w2[0], preferred_element_type=f32)
-        p2 += jnp.dot(feats[1, q, 1], w2[1], preferred_element_type=f32)
-        quarter[q, 0:128] = p01
-        quarter[q, 128:192] = p2[0:64] + pltpu.roll(p2[64:128], 64, 1)
-
-    lo, hi = pl.ds(0, 96), pl.ds(96, 96)
-    forward(z2)
-    c_a1 = put(quarter.at[z2, lo], rs_half.at[0], above)
-    c_b1 = put(quarter.at[z2, hi], rs_half.at[1], below)
-    forward(zu)
-    c_a2 = put(quarter.at[zu, hi], rs_full.at[0, hi], above)
-    forward(zd)
-    c_b2 = put(quarter.at[zd, lo], rs_full.at[1, lo], below)
-    forward(zh)
-    arrived(c_a1)
-    quarter[zu, 0:96] += rs_half[0]
-    c_a3 = put(quarter.at[zu, lo], rs_full.at[0, lo], above)
-    arrived(c_b1)
-    quarter[zd, 96:192] += rs_half[1]
-    c_b3 = put(quarter.at[zd, hi], rs_full.at[1, hi], below)
+    forward2(z2)
+    c_o2 = opposite(1)
+    c_d = [*direct(0)]
+    forward2(zu)
+    forward2(zd)
+    c_d += direct(1)
+    forward01(zh)
+    forward2(zh)
+    c_d += onward(0, *c_o1)
+    c_d += onward(1, *c_o2)
     for n in (0, 1):
         for q in range(4):
             for d in (0, 1):
                 block = feats[n, q, d].T.reshape(2, 320, 128)
                 featT[n, 2 * d : 2 * d + 2, :, 128 * q : 128 * q + 128] = block
-    arrived(c_a2, c_b2, c_a3, c_b3)
+    arrived(*c_d)
     if stop == 4:
         return finish()
 
@@ -215,13 +241,9 @@
     hidden = jnp.where(low[0:64], hidden[0:64], pltpu.roll(hidden[64:128], 64, 1))
     dcat[zh, 128:192] = hidden.astype(bf16)
 
-    c_a1, c_b1 = share(dcat.at[zh, lo], above), share(dcat.at[zh, hi], below)
-    c_a2, c_b2 = share(dcat.at[zh, hi], above), share(dcat.at[zh, lo], below)
-    arrived(c_a1)
-    c_a3 = share(dcat.at[zd, lo], above)
-    arrived(c_b1)
-    c_b3 = share(dcat.at[zu, hi], below)
-    arrived(c_a2, c_b2, c_a3, c_b3)
+    mine = dcat.at[zh]
+    c_a = [share(mine, to) for to in (opposed, above, below)]
+    arrived(*c_a)
     if stop == 5:
         return finish()
 
@@ -236,35 +258,44 @@
         p01 = jnp.dot(featT[0, v], d01, preferred_element_type=f32)
         p2 = jnp.dot(featT[1, v], d2, preferred_element_type=f32).reshape(4, 80, 128)
         rest = pltpu.roll(p2[:, 40:80].reshape(160, 128), 64, 1).reshape(4, 40, 128)
-        gbuf[v, :, 0:80] = p01.reshape(4, 80, 128)
-        gbuf[v, :, 80:120] = p2[:, 0:40] + rest
+        p01, p2 = p01.reshape(4, 80, 128), p2[:, 0:40] + rest
+        for n in range(4):
+            k = (n + 4 - z) % 4
+            gbuf[v, k, 0:80] = p01[n]
+            gbuf[v, k, 80:120] = p2[n]
 
     lo, hi = pl.ds(0, 2), pl.ds(2, 2)
     backward(flip(y2))
-    c_a1 = put(gbuf.at[flip(y2), lo], gy_half.at[0], up)
-    c_b1 = put(gbuf.at[flip(y2), hi], gy_half.at[1], down)
+    c_o = [
+        put(gbuf.at[flip(y2), k], gy_half.at[k], up if k < 2 else down) for k in range(4)
+    ]
     backward(flip(yu))
-    c_a2 = put(gbuf.at[flip(yu), hi], gy_full.at[0, hi], up)
+    c_d = [put(gbuf.at[flip(yu), hi], gy_full.at[0, hi], up)]
     backward(flip(yd))
-    c_b2 = put(gbuf.at[flip(yd), lo], gy_full.at[1, lo], down)
+    c_d.append(put(gbuf.at[flip(yd), lo], gy_full.at[1, lo], down))
     backward(flip(y))
-    arrived(c_a1)
-    gbuf[flip(yu), 0:2] += gy_half[0]
-    c_a3 = put(gbuf.at[flip(yu), lo], gy_full.at[0, lo], up)
-    arrived(c_b1)
-    gbuf[flip(yd), 2:4] += gy_half[1]
-    c_b3 = put(gbuf.at[flip(yd), hi], gy_full.at[1, hi], down)
-    arrived(c_a2, c_b2, c_a3, c_b3)
-    gline[...] = gbuf[flip(y)] + gy_full[0] + gy_full[1]
+    c_f = [None] * 4
+    for k in (1, 2, 3, 0):
+        arrived(c_o[k])
+        v = flip(yu) if k < 2 else flip(yd)
+        gbuf[v, k] += gy_half[k]
+        c_f[k] = put(gbuf.at[v, k], gy_full.at[k // 2, k], up if k < 2 else down)
+    arrived(*c_d)
+    c_z = []
+    for k in (1, 2, 3, 0):
+        arrived(c_f[k])
+        gline[k] = gbuf[flip(y), k] + gy_full[0, k] + gy_full[1, k]
+        if k > 0:
+            c_z.append(put(gline.at[k], gz_in.at[k - 1], skew[k - 1]))
     if stop == 6:
-        return finish()
-    c_z = [put(gline.at[(z + k) % 4], gz_in.at[k - 1], skew[k - 1]) for k in (1, 2, 3)]
+        arrived(*c_z)
+        return finish()
     arrived(*c_z)
-    gline[z] += gz_in[0] + gz_in[1] + gz_in[2]
+    gline[0] += gz_in[0] + gz_in[1] + gz_in[2]
     if stop == 7:
         return finish()
 
-    arrived(put(gline.at[z], gin, owners[0]))
+    arrived(put(gline.at[0], gin, owners[0]))
     if stop == 8:
         return finish()
 
@@ -287,37 +318,25 @@
             return fin.at[yy, xx, self.slots, pl.ds(start, size)]
 
         def begin(self):
-            mine = self.at(y, x)
-            self.r, self.l, self.u, self.d = (share(mine, to) for to in (right, left, up, down))
-            self.x2 = share(self.at(y, x, 0, 64), across_x)
-            self.y2 = share(self.at(y, x, 64, 64), across_y)
+            a, b = self.at(y, x, 0, 64), self.at(y, x, 64, 64)
+            self.ax = [share(a, to) for to in (right, left, across_x)]
+            self.by = [share(b, to) for to in (up, down, across_y)]
+            self.own = [share(a, up), share(b, right), share(a, down), share(b, left)]
 
         def turn(self):
-            def columns(xx):
-                return [share(self.at(y, xx, 0, 64), to) for to in (up, down)]
-
-            def rows(yy):
-                return [share(self.at(yy, x, 64, 64), to) for to in (right, left)]
-
-            arrived(self.r)
-            self.a = [columns(xd)]
-            self.last = [share(self.at(y, xd, 64, 32), right)]
-            arrived(self.u)
-            self.b = [rows(yd)]
-            self.last.append(share(self.at(yd, x, 0, 32), up))
-            arrived(self.l)
-            self.a.append(columns(xu))
-            self.last.append(share(self.at(y, xu, 96, 32), left))
-            arrived(self.d)
-            self.b.append(rows(yu))
-            self.last.append(share(self.at(yu, x, 32, 32), down))
-            arrived(self.x2)
-            self.a.append(columns(x2))
-            arrived(self.y2)
-            self.b.append(rows(y2))
+            self.a, self.b = [], []
+            for n, (xx, yy) in enumerate(((xd, yd), (xu, yu), (x2, y2))):
+                arrived(self.ax[n])
+                self.a.append([share(self.at(y, xx, 0, 64), to) for to in (up, down)])
+                arrived(self.by[n])
+                self.b.append([share(self.at(yy, x, 64, 64), to) for to in (right, left)])
 
         def forward(self):
-            for xx, yy, a, b in zip((xd, xu, x2), (yd, yu, y2), self.a, self.b):
+            self.last = []
+            au, br, ad, bl = self.own
+            pairs = [(x, y, (au, ad), (br, bl))]
+            pairs += zip((xd, xu, x2), (yd, yu, y2), self.a, self.b)
+            for xx, yy, a, b in pairs:
                 arrived(a[0])
                 self.last.append(share(self.at(yd, xx, 0, 32), up))
                 arrived(b[0])
@@ -388,12 +407,12 @@
             pltpu.VMEM((128, 128), bf16),
             pltpu.VMEM((4, 4, 128, 128), bf16),
             pltpu.VMEM((4, 192, 128), f32),
-            pltpu.VMEM((2, 96, 128), f32),
+            pltpu.VMEM((192, 128), f32),
             pltpu.VMEM((2, 192, 128), f32),
             pltpu.VMEM((4, 192, 128), bf16),
             pltpu.VMEM((2, 4, 320, 512), bf16),
             pltpu.VMEM((4, 4, 120, 128), f32),
-            pltpu.VMEM((2, 2, 120, 128), f32),
+            pltpu.VMEM((4, 120, 128), f32),
             pltpu.VMEM((2, 4, 120, 128), f32),
             pltpu.VMEM((4, 120, 128), f32),
             pltpu.VMEM((3, 120, 128), f32),

time: 115 us -> 111 us (0.965)
  Pallas kernels: 110 us -> 106 us
    pallas_call x1, Pallas kernels: 110 us -> 106 us  [local(): pl.pallas_call(functools.partial(kernel, stop), out_shape=(shard, jax.Sha...]
where the time goes in v4:
time: 111 us
  Pallas kernels  106 us (95%)
  local copies, waits for them, and re-layouts  2.94 us (3%)
  other arithmetic  1.78 us (2%)
    pallas_call x1, Pallas kernels, local(): pl.pallas_call(functools.partial(kernel, stop), out_shape=(shard, jax.Sha...  106 us
    unnamed x1, local copies, waits for them, and re-layouts  2.94 us

profile of v4, /device:TPU:64, one launch (start us, length us, event | category | flops | bytes accessed | tf_op | source)
XLA Modules:
  0.0 111.3 jit_solution(9194674576555198515)
XLA Ops:
  0.6 105.9 %fused_step.1 = (f32[3,64,80]{2,1,0:T(8,128)}, bf16[3,64,5120]{2,1,0:T(8,128)(2,1)}) custom-call(bf16[128,640]{1,0:T(8,128)(2,1)} %inputs_hbm.1, bf16[128,640]{1,0:T(8,128)(2,1)} %upstream_hbm.1, f32[3,64,80]{2,1,0:T(8,128)} %master_hbm.1, f32[3,64,80]{2,1,0:T(8,128)} %moment_one_hbm.1, f32[3,64,80]{2,1,0:T(8,128)} %moment_two_hbm.1), custom_call_target="tpu_custom_call" | custom-call | flops 503316480 | bytes 8000000 | tf_op jit(solution)/shard_map/fused_step/pallas_call | solution.py:398
  106.5 1.8 %multiply_subtract_fusion = (f32[3,64,80]{2,1,0:T(8,128)}, f32[3,64,80]{2,1,0:T(8,128)}, f32[3,64,80]{2,1,0:T(8,128)}) fusion(f32[3,64,80]{2,1,0:T(8,128)} %master_hbm.1, f32[3,64,80]{2,1,0:T(8,128)} %get-tuple-element.6, f32[3,64,80]{2,1,0:T(8,128)} %moment_one_hbm.1, f32[3,64,80]{2,1,0:T(8,128)} %moment_two_hbm.1), kind=kLoop, calls=%fused_computation.2 | loop fusion | flops 230400 | bytes 430080 | tf_op jit(solution)/shard_map/sub | solution.py:28
  108.3 2.9 %copy.10 = bf16[3,64,5120]{2,1,0:T(8,128)(2,1)} copy(bf16[3,64,5120]{2,1,0:T(8,128)(2,1)} %get-tuple-element.18) | data formatting | bytes 3932160

commit v5 on v4

--- a/solution.py
+++ b/solution.py
@@ -18,7 +18,7 @@
 MESH = pl.DeviceIdType.MESH
 f32 = jnp.float32
 bf16 = jnp.bfloat16
-N_COPIES = 160
+N_COPIES = 208
 
 
 def adamw(grads, master, moment_one, moment_two):
@@ -32,9 +32,9 @@
     stop,
     inputs_hbm, upstream_hbm, master_hbm, moment_one_hbm, moment_two_hbm,
     grads_out, weights_out,
-    feats, state, grads_own, wown, wbuf, quarter, rs_half, rs_full, dcat,
-    featT, gbuf, gy_half, gy_full, gline, gz_in, gin, fin, rows_new,
-    send_sems, recv_sems, load_sems, store_sems,
+    feats, state, wown, wbuf, quarter, rs_half, rs_full, dcat,
+    featT, gbuf, gy_half, gy_full, gline, gz_in, gin, fin,
+    send_sems, recv_sems, load_sems,
 ):
     i, j = lax.axis_index("dp"), lax.axis_index("mp")
     z, y, x = i // 16, (i // 4) % 4, i % 4
@@ -52,7 +52,7 @@
     line = [dev(z=(z + k) % 4) for k in (1, 2, 3)]
     skew = [dev(z=(z + k) % 4, x=(x + k) % 4) for k in (1, 2, 3)]
     above, below = dev(zh=zu), dev(zh=zd)
-    opposed, mate = dev(zh=z2), dev(core=1 - core)
+    mate = dev(core=1 - core)
     holders = [
         dev(zh=z, z=(x + m) % 4, y=flip(y), x=(zh + x + m) % 4) for m in range(4)
     ]
@@ -85,7 +85,7 @@
 
     barrier = pltpu.get_barrier_semaphore()
     greeted = [
-        *holders, *owners, above, below, opposed, *line, *skew,
+        *holders, *owners, above, below, *line, *skew,
         right, left, up, down, across_x, across_y, mate,
     ]
     for other in greeted:
@@ -241,9 +241,14 @@
     hidden = jnp.where(low[0:64], hidden[0:64], pltpu.roll(hidden[64:128], 64, 1))
     dcat[zh, 128:192] = hidden.astype(bf16)
 
-    mine = dcat.at[zh]
-    c_a = [share(mine, to) for to in (opposed, above, below)]
-    arrived(*c_a)
+    lo, hi = pl.ds(0, 96), pl.ds(96, 96)
+    c_a1, c_b1 = share(dcat.at[zh, lo], above), share(dcat.at[zh, hi], below)
+    c_a2, c_b2 = share(dcat.at[zh, hi], above), share(dcat.at[zh, lo], below)
+    arrived(c_a1)
+    c_a3 = share(dcat.at[zd, lo], above)
+    arrived(c_b1)
+    c_b3 = share(dcat.at[zu, hi], below)
+    arrived(c_a2, c_b2, c_a3, c_b3)
     if stop == 5:
         return finish()
 
@@ -306,9 +311,7 @@
     fin[y, x, 0] = shard_block(fresh.reshape(192, 80))
 
     c_z = [put(fin.at[y, x, 0], fin.at[y, x, 4 - k], line[k - 1]) for k in (1, 2, 3)]
-    grads_own[...] = grads
-    stores = [pltpu.make_async_copy(grads_own, grads_out, store_sems.at[0])]
-    stores[0].start()
+    grads_out[...] = grads
 
     class Plane:
         def __init__(self, slots):
@@ -351,59 +354,52 @@
 
     def unpack(r):
         n = (z + r) % 4
+        columns = pl.ds(pl.multiple_of(n * 1280, 128), 1280)
         both = fin[:, :, r, 0:80, :].reshape(1280, 128).T
-        rows_new[n, 0] = both[0:64]
-        rows_new[n, 1] = both[64:128]
+        weights_out[0, :, columns] = both[0:64]
+        weights_out[1, :, columns] = both[64:128]
         folded = fin[:, :, r, 80:128, :].reshape(768, 128).astype(f32)
         rest = pltpu.roll(folded, 64, 1).reshape(16, 48, 128)[:, 0:32]
         third = jnp.concatenate([folded.reshape(16, 48, 128), rest], axis=1)
-        rows_new[n, 2] = third.reshape(1280, 128).astype(bf16).T[0:64]
-        columns = pl.ds(pl.multiple_of(n * 1280, 128), 1280)
-        store = pltpu.make_async_copy(
-            rows_new.at[n], weights_out.at[:, :, columns], store_sems.at[1 + r]
-        )
-        store.start()
-        stores.append(store)
-
-    near, far = Plane(pl.ds(0, 1)), Plane(pl.ds(1, 3))
-    near.begin()
-    near.turn()
-    arrived(*c_z)
-    if stop == 9:
-        near.forward()
-        near.end()
-        stores[0].wait()
-        return finish()
-    far.begin()
-    near.forward()
-    far.turn()
-    near.end()
+        weights_out[2, :, columns] = third.reshape(1280, 128).astype(bf16).T[0:64]
+
+    one, two, rest = Plane(pl.ds(0, 1)), Plane(pl.ds(1, 1)), Plane(pl.ds(2, 2))
+    one.begin()
+    one.turn()
+    arrived(c_z[2])
+    two.begin()
+    one.forward()
+    arrived(c_z[0], c_z[1])
+    rest.begin()
+    two.turn()
+    one.end()
     unpack(0)
-    far.forward()
-    far.end()
+    rest.turn()
+    two.forward()
+    rest.forward()
+    two.end()
+    unpack(1)
+    rest.end()
     if stop == 10:
-        for store in stores:
-            store.wait()
-        return finish()
-    for r in (1, 2, 3):
-        unpack(r)
-    for store in stores:
-        store.wait()
+        return finish()
+    unpack(2)
+    unpack(3)
     finish()
 
 
 def local(stop, inputs, upstream, master, moment_one, moment_two):
-    shard = jax.ShapeDtypeStruct((3, 64, 80), f32)
     hbm = pl.BlockSpec(memory_space=pltpu.HBM)
+    vmem = pl.BlockSpec(memory_space=pltpu.VMEM)
+    operands = (inputs, upstream, master, moment_one, moment_two)
+    operands = [pltpu.with_memory_space_constraint(a, pltpu.HBM) for a in operands]
     grads, weights = pl.pallas_call(
         functools.partial(kernel, stop),
-        out_shape=(shard, jax.ShapeDtypeStruct((3, 64, 5120), bf16)),
+        out_shape=(pltpu.VMEM((3, 64, 80), f32), pltpu.VMEM((3, 64, 5120), bf16)),
         in_specs=[hbm] * 5,
-        out_specs=(hbm,) * 2,
+        out_specs=(vmem,) * 2,
         scratch_shapes=[
             pltpu.VMEM((2, 4, 2, 128, 640), bf16),
             pltpu.VMEM((3, 3, 64, 80), f32),
-            pltpu.VMEM((3, 64, 80), f32),
             pltpu.VMEM((128, 128), bf16),
             pltpu.VMEM((4, 4, 128, 128), bf16),
             pltpu.VMEM((4, 192, 128), f32),
@@ -418,20 +414,18 @@
             pltpu.VMEM((3, 120, 128), f32),
             pltpu.VMEM((120, 128), f32),
             pltpu.VMEM((4, 4, 4, 128, 128), bf16),
-            pltpu.VMEM((4, 3, 64, 1280), bf16),
             pltpu.SemaphoreType.DMA((N_COPIES,)),
             pltpu.SemaphoreType.DMA((N_COPIES,)),
             pltpu.SemaphoreType.DMA((5,)),
-            pltpu.SemaphoreType.DMA((5,)),
         ],
         compiler_params=pltpu.CompilerParams(
-            collective_id=0, has_side_effects=True, vmem_limit_bytes=62 * 2**20
+            collective_id=0, has_side_effects=True, vmem_limit_bytes=44 * 2**20
         ),
         cost_estimate=pl.CostEstimate(
             flops=503316480, bytes_accessed=8000000, transcendentals=8192
         ),
         name="fused_step",
-    )(inputs, upstream, master, moment_one, moment_two)
+    )(*operands)
     first, second, fresh = adamw(grads, master, moment_one, moment_two)
     return fresh, first, second, weights
 

time: 111 us -> 111 us (level)
  the two profiles are of different devices: /device:TPU:64 before, /device:TPU:32 now
where the time goes in v5:
time: 111 us
  Pallas kernels  107 us (96%)
  other arithmetic  1.74 us (2%)
  local copies, waits for them, and re-layouts  1.27 us (1%)
    pallas_call x1, Pallas kernels, local(): pl.pallas_call(functools.partial(kernel, stop), out_shape=(pltpu.VMEM((3,...  107 us

profile of v5, /device:TPU:32, one launch (start us, length us, event | category | flops | bytes accessed | tf_op | source)
XLA Modules:
  0.0 110.7 jit_solution(13193415484061166854)
XLA Ops:
  0.6 107.0 %fused_step.1 = (f32[3,64,80]{2,1,0:T(8,128)S(1)}, bf16[3,64,5120]{2,1,0:T(8,128)(2,1)S(1)}) custom-call(bf16[128,640]{1,0:T(8,128)(2,1)} %inputs_hbm.1, bf16[128,640]{1,0:T(8,128)(2,1)} %upstream_hbm.1, f32[3,64,80]{2,1,0:T(8,128)} %master_hbm.1, f32[3,64,80]{2,1,0:T(8,128)} %moment_one_hbm.1, f32[3,64,80]{2,1,0:T(8,128)} %moment_two_hbm.1), custom_call_target="tpu_custom_call" | custom-call | flops 503316480 | bytes 8000000 | tf_op jit(solution)/shard_map/fused_step/pallas_call | solution.py:395
  107.7 1.7 %multiply_subtract_fusion = (f32[3,64,80]{2,1,0:T(8,128)}, f32[3,64,80]{2,1,0:T(8,128)}, f32[3,64,80]{2,1,0:T(8,128)}) fusion(f32[3,64,80]{2,1,0:T(8,128)} %master_hbm.1, f32[3,64,80]{2,1,0:T(8,128)S(1)} %get-tuple-element.6, f32[3,64,80]{2,1,0:T(8,128)} %moment_one_hbm.1, f32[3,64,80]{2,1,0:T(8,128)} %moment_two_hbm.1), kind=kLoop, calls=%fused_computation.2 | loop fusion | flops 230400 | bytes 430080 | tf_op jit(solution)/shard_map/sub | solution.py:28
  109.4 1.3 %copy.10 = bf16[3,64,5120]{2,1,0:T(8,128)(2,1)} copy(bf16[3,64,5120]{2,1,0:T(8,128)(2,1)S(1)} %get-tuple-element.14) | data formatting | bytes 3932160

commit v6 on v5

--- a/solution.py
+++ b/solution.py
@@ -1,5 +1,3 @@
-import functools
-
 import jax
 import jax.numpy as jnp
 from jax import lax
@@ -29,7 +27,6 @@
 
 
 def kernel(
-    stop,
     inputs_hbm, upstream_hbm, master_hbm, moment_one_hbm, moment_two_hbm,
     grads_out, weights_out,
     feats, state, wown, wbuf, quarter, rs_half, rs_full, dcat,
@@ -159,9 +156,6 @@
     arrived(c_l2)
     c_m[1].append(share(feats.at[1, 2, core], mate))
     arrived(*c_m[0], *c_y[0])
-    if stop == 1:
-        arrived(*c_m[1], *c_y[1])
-        return finish()
 
     w01 = wbuf[:, :, 0:80, :].reshape(1280, 128)
     w01 = (w01[0:640], w01[640:1280])
@@ -225,8 +219,6 @@
                 block = feats[n, q, d].T.reshape(2, 320, 128)
                 featT[n, 2 * d : 2 * d + 2, :, 128 * q : 128 * q + 128] = block
     arrived(*c_d)
-    if stop == 4:
-        return finish()
 
     total = quarter[zh] + rs_full[0] + rs_full[1]
     gate = total[0:128]
@@ -249,8 +241,6 @@
     arrived(c_b1)
     c_b3 = share(dcat.at[zu, hi], below)
     arrived(c_a2, c_b2, c_a3, c_b3)
-    if stop == 5:
-        return finish()
 
     d01 = dcat[:, 0:128, :].reshape(512, 128)
     low = low_lanes(256)
@@ -292,17 +282,10 @@
         gline[k] = gbuf[flip(y), k] + gy_full[0, k] + gy_full[1, k]
         if k > 0:
             c_z.append(put(gline.at[k], gz_in.at[k - 1], skew[k - 1]))
-    if stop == 6:
-        arrived(*c_z)
-        return finish()
     arrived(*c_z)
     gline[0] += gz_in[0] + gz_in[1] + gz_in[2]
-    if stop == 7:
-        return finish()
 
     arrived(put(gline.at[0], gin, owners[0]))
-    if stop == 8:
-        return finish()
 
     g01 = gin[0:80]
     g2 = jnp.concatenate([gin[80:120], pltpu.roll(gin[80:120], 64, 1)], axis=0)
@@ -363,37 +346,29 @@
         third = jnp.concatenate([folded.reshape(16, 48, 128), rest], axis=1)
         weights_out[2, :, columns] = third.reshape(1280, 128).astype(bf16).T[0:64]
 
-    one, two, rest = Plane(pl.ds(0, 1)), Plane(pl.ds(1, 1)), Plane(pl.ds(2, 2))
-    one.begin()
-    one.turn()
-    arrived(c_z[2])
-    two.begin()
-    one.forward()
-    arrived(c_z[0], c_z[1])
-    rest.begin()
-    two.turn()
-    one.end()
+    near, far = Plane(pl.ds(0, 1)), Plane(pl.ds(1, 3))
+    near.begin()
+    near.turn()
+    arrived(*c_z)
+    far.begin()
+    near.forward()
+    far.turn()
+    near.end()
+    far.forward()
     unpack(0)
-    rest.turn()
-    two.forward()
-    rest.forward()
-    two.end()
-    unpack(1)
-    rest.end()
-    if stop == 10:
-        return finish()
-    unpack(2)
-    unpack(3)
+    far.end()
+    for r in (1, 2, 3):
+        unpack(r)
     finish()
 
 
-def local(stop, inputs, upstream, master, moment_one, moment_two):
+def local(inputs, upstream, master, moment_one, moment_two):
     hbm = pl.BlockSpec(memory_space=pltpu.HBM)
     vmem = pl.BlockSpec(memory_space=pltpu.VMEM)
     operands = (inputs, upstream, master, moment_one, moment_two)
     operands = [pltpu.with_memory_space_constraint(a, pltpu.HBM) for a in operands]
     grads, weights = pl.pallas_call(
-        functools.partial(kernel, stop),
+        kernel,
         out_shape=(pltpu.VMEM((3, 64, 80), f32), pltpu.VMEM((3, 64, 5120), bf16)),
         in_specs=[hbm] * 5,
         out_specs=(vmem,) * 2,
@@ -430,10 +405,10 @@
     return fresh, first, second, weights
 
 
-def solution(mesh, stop=0):
+def solution(mesh):
     owned = P(None, "mp", "dp")
     return jax.shard_map(
-        functools.partial(local, stop),
+        local,
         mesh=mesh,
         in_specs=(P("dp", "mp"), P("dp", "mp"), owned, owned, owned),
         out_specs=(owned, owned, owned, P(None, "mp", None)),

time: 111 us -> 108 us (0.973)
  Pallas kernels: 107 us -> 105 us
    pallas_call x1, Pallas kernels: 107 us -> 105 us  [local(): pl.pallas_call(kernel, out_shape=(pltpu.VMEM((3, 64, 80), f32), pltpu.VME...]
where the time goes in v6:
time: 108 us
  Pallas kernels  105 us (97%)
  other arithmetic  1.74 us (2%)
  local copies, waits for them, and re-layouts  1.27 us (1%)
    pallas_call x1, Pallas kernels, local(): pl.pallas_call(kernel, out_shape=(pltpu.VMEM((3, 64, 80), f32), pltpu.VME...  105 us

profile of v6, /device:TPU:32, one launch (start us, length us, event | category | flops | bytes accessed | tf_op | source)
XLA Modules:
  0.0 108.3 jit_solution(3386163128730793367)
XLA Ops:
  0.6 104.6 %fused_step.1 = (f32[3,64,80]{2,1,0:T(8,128)S(1)}, bf16[3,64,5120]{2,1,0:T(8,128)(2,1)S(1)}) custom-call(bf16[128,640]{1,0:T(8,128)(2,1)} %inputs_hbm.1, bf16[128,640]{1,0:T(8,128)(2,1)} %upstream_hbm.1, f32[3,64,80]{2,1,0:T(8,128)} %master_hbm.1, f32[3,64,80]{2,1,0:T(8,128)} %moment_one_hbm.1, f32[3,64,80]{2,1,0:T(8,128)} %moment_two_hbm.1), custom_call_target="tpu_custom_call" | custom-call | flops 503316480 | bytes 8000000 | tf_op jit(solution)/shard_map/fused_step/pallas_call | solution.py:370
  105.3 1.7 %multiply_subtract_fusion = (f32[3,64,80]{2,1,0:T(8,128)}, f32[3,64,80]{2,1,0:T(8,128)}, f32[3,64,80]{2,1,0:T(8,128)}) fusion(f32[3,64,80]{2,1,0:T(8,128)} %master_hbm.1, f32[3,64,80]{2,1,0:T(8,128)S(1)} %get-tuple-element.6, f32[3,64,80]{2,1,0:T(8,128)} %moment_one_hbm.1, f32[3,64,80]{2,1,0:T(8,128)} %moment_two_hbm.1), kind=kLoop, calls=%fused_computation.2 | loop fusion | flops 230400 | bytes 430080 | tf_op jit(solution)/shard_map/sub | solution.py:26
  107.0 1.3 %copy.10 = bf16[3,64,5120]{2,1,0:T(8,128)(2,1)} copy(bf16[3,64,5120]{2,1,0:T(8,128)(2,1)S(1)} %get-tuple-element.14) | data formatting | bytes 3932160

commit v7 on v6

--- a/solution.py
+++ b/solution.py
@@ -205,87 +205,134 @@
     w2 = (w2[0:640], w2[640:1280])
     forward2(z2)
     c_o2 = opposite(1)
-    c_d = [*direct(0)]
+    c_d = [direct(0)]
     forward2(zu)
     forward2(zd)
-    c_d += direct(1)
+    c_d.append(direct(1))
     forward01(zh)
     forward2(zh)
-    c_d += onward(0, *c_o1)
-    c_d += onward(1, *c_o2)
+    c_d[0] += onward(0, *c_o1)
+    c_d[1] += onward(1, *c_o2)
     for n in (0, 1):
         for q in range(4):
             for d in (0, 1):
                 block = feats[n, q, d].T.reshape(2, 320, 128)
                 featT[n, 2 * d : 2 * d + 2, :, 128 * q : 128 * q + 128] = block
-    arrived(*c_d)
-
-    total = quarter[zh] + rs_full[0] + rs_full[1]
-    gate = total[0:128]
+
+    def summed(n, rows):
+        arrived(*c_d[n])
+        return quarter[zh, rows] + rs_full[0, rows] + rs_full[1, rows]
+
+    def gather(n):
+        mine, a, b = dcat.at[zh], lo[n], hi[n]
+        pairs = ((a, above), (b, below), (b, above), (a, below))
+        return [share(mine.at[rows], to) for rows, to in pairs]
+
+    def pass_on(n, copies):
+        arrived(copies[0])
+        c_a = share(dcat.at[zd, lo[n]], above)
+        arrived(copies[1])
+        return [c_a, share(dcat.at[zu, hi[n]], below)]
+
+    low = low_lanes(128)
+    gate = summed(0, slice(0, 128))
     upval = pltpu.roll(gate, 64, 1)
-    dhidden = jnp.concatenate([total[128:192], pltpu.roll(total[128:192], 64, 1)], axis=0)
     sigma = jax.nn.sigmoid(gate)
     hidden = gate * sigma * upval
+    hidden = jnp.where(low[0:64], hidden[0:64], pltpu.roll(hidden[64:128], 64, 1))
+    dcat[zh, 128:192] = hidden.astype(bf16)
+    c_h = gather(1)
+    folded = summed(1, slice(128, 192))
+    dhidden = jnp.concatenate([folded, pltpu.roll(folded, 64, 1)], axis=0)
     dgate = dhidden * upval * sigma * (1.0 + gate * (1.0 - sigma))
     dup = dhidden * gate * sigma
-    low = low_lanes(128)
     dcat[zh, 0:128] = jnp.where(low, dgate, pltpu.roll(dup, 64, 1)).astype(bf16)
-    hidden = jnp.where(low[0:64], hidden[0:64], pltpu.roll(hidden[64:128], 64, 1))
-    dcat[zh, 128:192] = hidden.astype(bf16)
-
-    lo, hi = pl.ds(0, 96), pl.ds(96, 96)
-    c_a1, c_b1 = share(dcat.at[zh, lo], above), share(dcat.at[zh, hi], below)
-    c_a2, c_b2 = share(dcat.at[zh, hi], above), share(dcat.at[zh, lo], below)
-    arrived(c_a1)
-    c_a3 = share(dcat.at[zd, lo], above)
-    arrived(c_b1)
-    c_b3 = share(dcat.at[zu, hi], below)
-    arrived(c_a2, c_b2, c_a3, c_b3)
-
-    d01 = dcat[:, 0:128, :].reshape(512, 128)
+    c_g = gather(0)
+    c_h = c_h[2:] + pass_on(1, c_h)
+    c_g = c_g[2:] + pass_on(0, c_g)
+
+    lo, hi = pl.ds(0, 2), pl.ds(2, 2)
+    wide, down_rows = pl.ds(0, 80), pl.ds(80, 40)
+
+    def store(v, rows, values):
+        for n in range(4):
+            gbuf[v, (n + 4 - z) % 4, rows] = values[n]
+
+    arrived(*c_h)
     low = low_lanes(256)
     folded = dcat[:, 128:192, :].reshape(256, 128).astype(f32)
     early = jnp.where(low, folded, 0.0).astype(bf16).reshape(4, 64, 128)
     late = jnp.where(low, pltpu.roll(folded, 64, 1), 0.0).astype(bf16).reshape(4, 64, 128)
     d2 = jnp.concatenate([early, late], axis=1).reshape(512, 128)
 
-    def backward(v):
-        p01 = jnp.dot(featT[0, v], d01, preferred_element_type=f32)
+    def backward2(v):
         p2 = jnp.dot(featT[1, v], d2, preferred_element_type=f32).reshape(4, 80, 128)
         rest = pltpu.roll(p2[:, 40:80].reshape(160, 128), 64, 1).reshape(4, 40, 128)
-        p01, p2 = p01.reshape(4, 80, 128), p2[:, 0:40] + rest
-        for n in range(4):
-            k = (n + 4 - z) % 4
-            gbuf[v, k, 0:80] = p01[n]
-            gbuf[v, k, 80:120] = p2[n]
-
-    lo, hi = pl.ds(0, 2), pl.ds(2, 2)
-    backward(flip(y2))
+        store(v, down_rows, p2[:, 0:40] + rest)
+
+    backward2(flip(y2))
+    h_o = [
+        put(gbuf.at[flip(y2), lo, down_rows], gy_half.at[lo, down_rows], up),
+        put(gbuf.at[flip(y2), hi, down_rows], gy_half.at[hi, down_rows], down),
+    ]
+    backward2(flip(yu))
+    backward2(flip(yd))
+    h_d = [
+        put(gbuf.at[flip(yu), hi, down_rows], gy_full.at[0, hi, down_rows], up),
+        put(gbuf.at[flip(yd), lo, down_rows], gy_full.at[1, lo, down_rows], down),
+    ]
+    backward2(flip(y))
+
+    arrived(*c_g)
+    d01 = dcat[:, 0:128, :].reshape(512, 128)
+
+    def backward01(v):
+        p01 = jnp.dot(featT[0, v], d01, preferred_element_type=f32)
+        store(v, wide, p01.reshape(4, 80, 128))
+
+    backward01(flip(y2))
     c_o = [
-        put(gbuf.at[flip(y2), k], gy_half.at[k], up if k < 2 else down) for k in range(4)
-    ]
-    backward(flip(yu))
-    c_d = [put(gbuf.at[flip(yu), hi], gy_full.at[0, hi], up)]
-    backward(flip(yd))
-    c_d.append(put(gbuf.at[flip(yd), lo], gy_full.at[1, lo], down))
-    backward(flip(y))
+        put(gbuf.at[flip(y2), k, wide], gy_half.at[k, wide], up if k < 2 else down)
+        for k in range(4)
+    ]
+    backward01(flip(yu))
+    c_d = [put(gbuf.at[flip(yu), hi, wide], gy_full.at[0, hi, wide], up)]
+    backward01(flip(yd))
+    c_d.append(put(gbuf.at[flip(yd), lo, wide], gy_full.at[1, lo, wide], down))
+    arrived(h_o[0])
+    gbuf[flip(yu), lo, down_rows] += gy_half[lo, down_rows]
+    h_d.append(put(gbuf.at[flip(yu), lo, down_rows], gy_full.at[0, lo, down_rows], up))
+    arrived(h_o[1])
+    gbuf[flip(yd), hi, down_rows] += gy_half[hi, down_rows]
+    h_d.append(put(gbuf.at[flip(yd), hi, down_rows], gy_full.at[1, hi, down_rows], down))
+    backward01(flip(y))
     c_f = [None] * 4
     for k in (1, 2, 3, 0):
         arrived(c_o[k])
         v = flip(yu) if k < 2 else flip(yd)
-        gbuf[v, k] += gy_half[k]
-        c_f[k] = put(gbuf.at[v, k], gy_full.at[k // 2, k], up if k < 2 else down)
+        gbuf[v, k, wide] += gy_half[k, wide]
+        dst = gy_full.at[k // 2, k, wide]
+        c_f[k] = put(gbuf.at[v, k, wide], dst, up if k < 2 else down)
+
+    def along(k, rows):
+        gline[k, rows] = gbuf[flip(y), k, rows] + gy_full[0, k, rows] + gy_full[1, k, rows]
+        if k > 0:
+            return put(gline.at[k, rows], gz_in.at[k - 1, rows], skew[k - 1])
+
+    def home(copies, rows):
+        arrived(*copies)
+        gline[0, rows] += gz_in[0, rows] + gz_in[1, rows] + gz_in[2, rows]
+        return put(gline.at[0, rows], gin.at[rows], owners[0])
+
+    arrived(*h_d)
+    h_z = [along(k, down_rows) for k in (1, 2, 3, 0)][:3]
     arrived(*c_d)
     c_z = []
     for k in (1, 2, 3, 0):
         arrived(c_f[k])
-        gline[k] = gbuf[flip(y), k] + gy_full[0, k] + gy_full[1, k]
-        if k > 0:
-            c_z.append(put(gline.at[k], gz_in.at[k - 1], skew[k - 1]))
-    arrived(*c_z)
-    gline[0] += gz_in[0] + gz_in[1] + gz_in[2]
-
-    arrived(put(gline.at[0], gin, owners[0]))
+        c_z.append(along(k, wide))
+    c_home = [home(h_z, down_rows), home(c_z[:3], wide)]
+    arrived(*c_home)
 
     g01 = gin[0:80]
     g2 = jnp.concatenate([gin[80:120], pltpu.roll(gin[80:120], 64, 1)], axis=0)

time: 108 us -> 107 us (level)
  the two profiles are of different devices: /device:TPU:32 before, /device:TPU:64 now
where the time goes in v7:
time: 107 us
  Pallas kernels  103 us (96%)
  other arithmetic  1.74 us (2%)
  local copies, waits for them, and re-layouts  1.27 us (1%)
    pallas_call x1, Pallas kernels, local(): pl.pallas_call(kernel, out_shape=(pltpu.VMEM((3, 64, 80), f32), pltpu.VME...  103 us

profile of v7, /device:TPU:64, one launch (start us, length us, event | category | flops | bytes accessed | tf_op | source)
XLA Modules:
  0.0 107.0 jit_solution(10757109061884008297)
XLA Ops:
  0.6 103.4 %fused_step.1 = (f32[3,64,80]{2,1,0:T(8,128)S(1)}, bf16[3,64,5120]{2,1,0:T(8,128)(2,1)S(1)}) custom-call(bf16[128,640]{1,0:T(8,128)(2,1)} %inputs_hbm.1, bf16[128,640]{1,0:T(8,128)(2,1)} %upstream_hbm.1, f32[3,64,80]{2,1,0:T(8,128)} %master_hbm.1, f32[3,64,80]{2,1,0:T(8,128)} %moment_one_hbm.1, f32[3,64,80]{2,1,0:T(8,128)} %moment_two_hbm.1), custom_call_target="tpu_custom_call" | custom-call | flops 503316480 | bytes 8000000 | tf_op jit(solution)/shard_map/fused_step/pallas_call | solution.py:417
  104.0 1.7 %multiply_subtract_fusion = (f32[3,64,80]{2,1,0:T(8,128)}, f32[3,64,80]{2,1,0:T(8,128)}, f32[3,64,80]{2,1,0:T(8,128)}) fusion(f32[3,64,80]{2,1,0:T(8,128)} %master_hbm.1, f32[3,64,80]{2,1,0:T(8,128)S(1)} %get-tuple-element.6, f32[3,64,80]{2,1,0:T(8,128)} %moment_one_hbm.1, f32[3,64,80]{2,1,0:T(8,128)} %moment_two_hbm.1), kind=kLoop, calls=%fused_computation.2 | loop fusion | flops 230400 | bytes 430080 | tf_op jit(solution)/shard_map/sub | solution.py:26
  105.7 1.3 %copy.10 = bf16[3,64,5120]{2,1,0:T(8,128)(2,1)} copy(bf16[3,64,5120]{2,1,0:T(8,128)(2,1)S(1)} %get-tuple-element.14) | data formatting | bytes 3932160

commit v8 on v7

--- a/solution.py
+++ b/solution.py
@@ -135,26 +135,22 @@
         piece = wbuf.at[flip(y), (z + 4 - m) % 4, (gate_up, down_part)[n]]
         c_y[n].extend(share(piece, to) for to in (up, down, across_y))
 
-    spread(0, 0)
-    spread(0, 1)
     arrived(c_r[0])
     c_r2 = put(feats.at[0, 3, core], feats.at[0, 2, core], right)
     c_m[0].append(share(feats.at[0, 3, core], mate))
-    spread(0, 2)
-    spread(0, 3)
     arrived(c_l[0])
     c_m[0].append(share(feats.at[0, 1, core], mate))
+    for m in range(4):
+        spread(0, m)
     arrived(c_l[1])
     c_l2 = put(feats.at[1, 1, core], feats.at[1, 2, core], left)
     c_m[1].append(share(feats.at[1, 1, core], mate))
     for m in range(4):
         spread(1, m)
+    arrived(c_r2)
+    c_m[0].append(share(feats.at[0, 2, core], mate))
     arrived(c_r[1])
     c_m[1].append(share(feats.at[1, 3, core], mate))
-    arrived(c_r2)
-    c_m[0].append(share(feats.at[0, 2, core], mate))
-    arrived(c_l2)
-    c_m[1].append(share(feats.at[1, 2, core], mate))
     arrived(*c_m[0], *c_y[0])
 
     w01 = wbuf[:, :, 0:80, :].reshape(1280, 128)
@@ -196,6 +192,8 @@
     c_o1 = opposite(0)
     forward01(zu)
     forward01(zd)
+    arrived(c_l2)
+    c_m[1].append(share(feats.at[1, 2, core], mate))
     arrived(*c_m[1], *c_y[1])
     folded = wbuf[:, :, 80:128, :].reshape(768, 128).astype(f32)
     low = low_lanes(768)
@@ -379,6 +377,17 @@
                 arrived(b[1])
                 self.last.append(share(self.at(yy, xu, 96, 32), left))
 
+        def forward_whole(self):
+            au, br, ad, bl = self.own
+            arrived(au, *(a[0] for a in self.a))
+            self.last = [share(fin.at[yd, :, self.slots, pl.ds(0, 32)], up)]
+            arrived(br, *(b[0] for b in self.b))
+            self.last.append(share(fin.at[:, xd, self.slots, pl.ds(64, 32)], right))
+            arrived(ad, *(a[1] for a in self.a))
+            self.last.append(share(fin.at[yu, :, self.slots, pl.ds(32, 32)], down))
+            arrived(bl, *(b[1] for b in self.b))
+            self.last.append(share(fin.at[:, xu, self.slots, pl.ds(96, 32)], left))
+
         def end(self):
             arrived(*self.last)
 
@@ -398,10 +407,10 @@
     near.turn()
     arrived(*c_z)
     far.begin()
-    near.forward()
     far.turn()
+    near.forward_whole()
+    far.forward()
     near.end()
-    far.forward()
     unpack(0)
     far.end()
     for r in (1, 2, 3):

time: 107 us -> 107 us (level)
  the two profiles are of different devices: /device:TPU:64 before, /device:TPU:32 now
where the time goes in v8:
time: 107 us
  Pallas kernels  103 us (96%)
  other arithmetic  1.74 us (2%)
  local copies, waits for them, and re-layouts  1.27 us (1%)
    pallas_call x1, Pallas kernels, local(): pl.pallas_call(kernel, out_shape=(pltpu.VMEM((3, 64, 80), f32), pltpu.VME...  103 us

profile of v8, /device:TPU:32, one launch (start us, length us, event | category | flops | bytes accessed | tf_op | source)
XLA Modules:
  0.0 106.7 jit_solution(6814770230148278228)
XLA Ops:
  0.6 103.1 %fused_step.1 = (f32[3,64,80]{2,1,0:T(8,128)S(1)}, bf16[3,64,5120]{2,1,0:T(8,128)(2,1)S(1)}) custom-call(bf16[128,640]{1,0:T(8,128)(2,1)} %inputs_hbm.1, bf16[128,640]{1,0:T(8,128)(2,1)} %upstream_hbm.1, f32[3,64,80]{2,1,0:T(8,128)} %master_hbm.1, f32[3,64,80]{2,1,0:T(8,128)} %moment_one_hbm.1, f32[3,64,80]{2,1,0:T(8,128)} %moment_two_hbm.1), custom_call_target="tpu_custom_call" | custom-call | flops 503316480 | bytes 8000000 | tf_op jit(solution)/shard_map/fused_step/pallas_call | solution.py:426
  103.7 1.7 %multiply_subtract_fusion = (f32[3,64,80]{2,1,0:T(8,128)}, f32[3,64,80]{2,1,0:T(8,128)}, f32[3,64,80]{2,1,0:T(8,128)}) fusion(f32[3,64,80]{2,1,0:T(8,128)} %master_hbm.1, f32[3,64,80]{2,1,0:T(8,128)S(1)} %get-tuple-element.6, f32[3,64,80]{2,1,0:T(8,128)} %moment_one_hbm.1, f32[3,64,80]{2,1,0:T(8,128)} %moment_two_hbm.1), kind=kLoop, calls=%fused_computation.2 | loop fusion | flops 230400 | bytes 430080 | tf_op jit(solution)/shard_map/sub | solution.py:26
  105.5 1.3 %copy.10 = bf16[3,64,5120]{2,1,0:T(8,128)(2,1)} copy(bf16[3,64,5120]{2,1,0:T(8,128)(2,1)S(1)} %get-tuple-element.14) | data formatting | bytes 3932160

commit v9 on v8

--- a/solution.py
+++ b/solution.py
@@ -28,7 +28,7 @@
 
 def kernel(
     inputs_hbm, upstream_hbm, master_hbm, moment_one_hbm, moment_two_hbm,
-    grads_out, weights_out,
+    fresh_out, first_out, second_out, weights_out,
     feats, state, wown, wbuf, quarter, rs_half, rs_full, dcat,
     featT, gbuf, gy_half, gy_full, gline, gz_in, gin, fin,
     send_sems, recv_sems, load_sems,
@@ -335,11 +335,13 @@
     g01 = gin[0:80]
     g2 = jnp.concatenate([gin[80:120], pltpu.roll(gin[80:120], 64, 1)], axis=0)
     grads = jnp.concatenate([g01.T, g2.T[0:64]], axis=0).reshape(3, 64, 80)
-    fresh = adamw(grads, state[0], state[1], state[2])[2]
+    first, second, fresh = adamw(grads, state[0], state[1], state[2])
     fin[y, x, 0] = shard_block(fresh.reshape(192, 80))
 
     c_z = [put(fin.at[y, x, 0], fin.at[y, x, 4 - k], line[k - 1]) for k in (1, 2, 3)]
-    grads_out[...] = grads
+    fresh_out[...] = fresh
+    first_out[...] = first
+    second_out[...] = second
 
     class Plane:
         def __init__(self, slots):
@@ -418,16 +420,27 @@
     finish()
 
 
+def write_back(*refs):
+    sources, targets, sems = refs[0:4], refs[4:8], refs[8]
+    copies = [
+        pltpu.make_async_copy(sources[k], targets[k], sems.at[k]) for k in (3, 0, 1, 2)
+    ]
+    for copy in copies:
+        copy.start()
+    for copy in copies:
+        copy.wait()
+
+
 def local(inputs, upstream, master, moment_one, moment_two):
     hbm = pl.BlockSpec(memory_space=pltpu.HBM)
     vmem = pl.BlockSpec(memory_space=pltpu.VMEM)
     operands = (inputs, upstream, master, moment_one, moment_two)
     operands = [pltpu.with_memory_space_constraint(a, pltpu.HBM) for a in operands]
-    grads, weights = pl.pallas_call(
+    results = pl.pallas_call(
         kernel,
-        out_shape=(pltpu.VMEM((3, 64, 80), f32), pltpu.VMEM((3, 64, 5120), bf16)),
+        out_shape=(*(pltpu.VMEM((3, 64, 80), f32),) * 3, pltpu.VMEM((3, 64, 5120), bf16)),
         in_specs=[hbm] * 5,
-        out_specs=(vmem,) * 2,
+        out_specs=(vmem,) * 4,
         scratch_shapes=[
             pltpu.VMEM((2, 4, 2, 128, 640), bf16),
             pltpu.VMEM((3, 3, 64, 80), f32),
@@ -457,8 +470,16 @@
         ),
         name="fused_step",
     )(*operands)
-    first, second, fresh = adamw(grads, master, moment_one, moment_two)
-    return fresh, first, second, weights
+    results = [pltpu.with_memory_space_constraint(a, pltpu.VMEM) for a in results]
+    return pl.pallas_call(
+        write_back,
+        out_shape=tuple(jax.ShapeDtypeStruct(a.shape, a.dtype) for a in results),
+        in_specs=[vmem] * 4,
+        out_specs=(hbm,) * 4,
+        scratch_shapes=[pltpu.SemaphoreType.DMA((4,))],
+        cost_estimate=pl.CostEstimate(flops=0, bytes_accessed=4500000, transcendentals=0),
+        name="write_back",
+    )(*results)
 
 
 def solution(mesh):

time: 107 us -> 106 us (level)
  the two profiles are of different devices: /device:TPU:32 before, /device:TPU:64 now
where the time goes in v9:
time: 106 us
  Pallas kernels  105 us (99%)
    pallas_call x1, Pallas kernels, local(): pl.pallas_call(kernel, out_shape=(*(pltpu.VMEM((3, 64, 80), f32),) * 3, p...  104 us

profile of v9, /device:TPU:64, one launch (start us, length us, event | category | flops | bytes accessed | tf_op | source)
XLA Modules:
  0.0 105.6 jit_solution(11504021819666504503)
XLA Ops:
  0.6 103.6 %fused_step.1 = (f32[3,64,80]{2,1,0:T(8,128)S(1)}, f32[3,64,80]{2,1,0:T(8,128)S(1)}, f32[3,64,80]{2,1,0:T(8,128)S(1)}, bf16[3,64,5120]{2,1,0:T(8,128)(2,1)S(1)}) custom-call(bf16[128,640]{1,0:T(8,128)(2,1)} %inputs_hbm.1, bf16[128,640]{1,0:T(8,128)(2,1)} %upstream_hbm.1, f32[3,64,80]{2,1,0:T(8,128)} %master_hbm.1, f32[3,64,80]{2,1,0:T(8,128)} %moment_one_hbm.1, ...), custom_call_target="tpu_custom_call" | custom-call | flops 503316480 | bytes 8000000 | tf_op jit(solution)/shard_map/fused_step/pallas_call | solution.py:439
  104.2 1.4 %write_back.1 = (f32[3,64,80]{2,1,0:T(8,128)}, f32[3,64,80]{2,1,0:T(8,128)}, f32[3,64,80]{2,1,0:T(8,128)}, bf16[3,64,5120]{2,1,0:T(8,128)(2,1)}) custom-call(f32[3,64,80]{2,1,0:T(8,128)S(1)} %get-tuple-element.8.refs_0_, f32[3,64,80]{2,1,0:T(8,128)S(1)} %get-tuple-element.9.refs_1_, f32[3,64,80]{2,1,0:T(8,128)S(1)} %get-tuple-element.10.refs_2_, ...), custom_call_target="tpu_custom_call" | custom-call | bytes 4500000 | tf_op jit(solution)/shard_map/write_back/pallas_call | solution.py:474

commit v10 on v9

--- a/solution.py
+++ b/solution.py
@@ -82,7 +82,7 @@
 
     barrier = pltpu.get_barrier_semaphore()
     greeted = [
-        *holders, *owners, above, below, *line, *skew,
+        *owners, *holders, above, below, *line, *skew,
         right, left, up, down, across_x, across_y, mate,
     ]
     for other in greeted:
@@ -132,7 +132,7 @@
 
     def spread(n, m):
         arrived(c_w[n][m])
-        piece = wbuf.at[flip(y), (z + 4 - m) % 4, (gate_up, down_part)[n]]
+        piece = wbuf.at[flip(y), (z + 4 - m) % 4, gate_up]
         c_y[n].extend(share(piece, to) for to in (up, down, across_y))
 
     arrived(c_r[0])
@@ -140,13 +140,15 @@
     c_m[0].append(share(feats.at[0, 3, core], mate))
     arrived(c_l[0])
     c_m[0].append(share(feats.at[0, 1, core], mate))
-    for m in range(4):
-        spread(0, m)
+    spread(0, 0)
+    spread(0, 1)
     arrived(c_l[1])
     c_l2 = put(feats.at[1, 1, core], feats.at[1, 2, core], left)
     c_m[1].append(share(feats.at[1, 1, core], mate))
-    for m in range(4):
-        spread(1, m)
+    spread(0, 2)
+    spread(0, 3)
+    arrived(*c_w[1])
+    c_y[1] = [share(wbuf.at[flip(y), :, down_part], to) for to in (up, down, across_y)]
     arrived(c_r2)
     c_m[0].append(share(feats.at[0, 2, core], mate))
     arrived(c_r[1])

time: 106 us -> 106 us (level)
  the two profiles are of different devices: /device:TPU:64 before, /device:TPU:32 now
where the time goes in v10:
time: 106 us
  Pallas kernels  105 us (99%)
    pallas_call x1, Pallas kernels, local(): pl.pallas_call(kernel, out_shape=(*(pltpu.VMEM((3, 64, 80), f32),) * 3, p...  103 us

profile of v10, /device:TPU:32, one launch (start us, length us, event | category | flops | bytes accessed | tf_op | source)
XLA Modules:
  0.0 105.5 jit_solution(6610175923321412208)
XLA Ops:
  0.6 103.5 %fused_step.1 = (f32[3,64,80]{2,1,0:T(8,128)S(1)}, f32[3,64,80]{2,1,0:T(8,128)S(1)}, f32[3,64,80]{2,1,0:T(8,128)S(1)}, bf16[3,64,5120]{2,1,0:T(8,128)(2,1)S(1)}) custom-call(bf16[128,640]{1,0:T(8,128)(2,1)} %inputs_hbm.1, bf16[128,640]{1,0:T(8,128)(2,1)} %upstream_hbm.1, f32[3,64,80]{2,1,0:T(8,128)} %master_hbm.1, f32[3,64,80]{2,1,0:T(8,128)} %moment_one_hbm.1, ...), custom_call_target="tpu_custom_call" | custom-call | flops 503316480 | bytes 8000000 | tf_op jit(solution)/shard_map/fused_step/pallas_call | solution.py:441
  104.1 1.4 %write_back.1 = (f32[3,64,80]{2,1,0:T(8,128)}, f32[3,64,80]{2,1,0:T(8,128)}, f32[3,64,80]{2,1,0:T(8,128)}, bf16[3,64,5120]{2,1,0:T(8,128)(2,1)}) custom-call(f32[3,64,80]{2,1,0:T(8,128)S(1)} %get-tuple-element.8.refs_0_, f32[3,64,80]{2,1,0:T(8,128)S(1)} %get-tuple-element.9.refs_1_, f32[3,64,80]{2,1,0:T(8,128)S(1)} %get-tuple-element.10.refs_2_, ...), custom_call_target="tpu_custom_call" | custom-call | bytes 4500000 | tf_op jit(solution)/shard_map/write_back/pallas_call | solution.py:476
